TPU v7x, 256 devices: a whole 4x4x8 slice. The times are simulated.
256 devices in a mesh: seq: 16 (over y, x), mp: 8 (over z), dp: 2 (over core).
Axes of the slice: x: 4, y: 4, z: 8, core: 2. Of those that a mesh axis runs over, the one named last changes fastest.
Arguments:
- queries: bfloat16 [2, 4096, 4096], P('dp', 'seq', 'mp'), may hold values from -8 to 8
- encodings: bfloat16 [2, 2, 256, 128, 4096], P('dp', None, 'seq', None, 'mp'), may hold values from -8 to 8
- sink: float32 [32], P('mp'), may hold values from 1 to 6
- owner: int32 [2, 128], P('dp'), may hold values from 0 to 15, as said below
- doc_start: int32 [2, 64], P('dp'), may hold values 0 or 1
- d_out: bfloat16 [2, 4096, 4096], P('dp', 'seq', 'mp'), may hold values from -8 to 8
Outputs:
- attended: bfloat16 [2, 4096, 4096], P('dp', 'seq', 'mp')
- d_queries: bfloat16 [2, 4096, 4096], P('dp', 'seq', 'mp')
- d_encodings: bfloat16 [2, 2, 256, 128, 4096], P('dp', None, 'seq', None, 'mp')
- d_sink: float32 [32], P('mp')
Inputs may be any that keep to these rules, and one draw needn't show every extreme that they name: `owner`: neighbour n belongs to span n // 2. One encoder group holds at most 16 neighbours of a sample, and some group exactly 16; of the neighbours of any 4 consecutive spans at most 2 are held by one group, and exactly 2 in some aligned block of 4 spans.
All inputs are finite; a program needn't handle non-finite values. No bound on the sum of `doc_start` on one device may be relied on, other than what follows from the above.
Results may differ from a plain program's by a relative error of at most 0.011.
Values may be sent and summed in bfloat16 or wider, within the bound.
No kernel may reach another device: no remote copies, remote signals or barrier semaphores. Data moves between devices by JAX's collectives and lax.ppermute only.
A program may use at most 128 MiB of HBM per device.

v0:
```python
import jax
import jax.numpy as jnp
from jax import lax
from jax.sharding import PartitionSpec as P

HD = 128
CH = 64
NB = 2
NL = 128
PAIR_CAP = 2


def from_behind(block, axis, distance):
    devices = range(lax.axis_size(axis))
    route = [(i - distance, i) for i in devices if i - distance in devices]
    return lax.ppermute(block, axis, route)


def routing(owner_row, seq_index, seq_count, spans_here, enc_cap, lead_spans):
    neigh_count = owner_row.shape[0]
    neigh_ids = jnp.arange(neigh_count, dtype=jnp.int32)
    dest_dev = (neigh_ids // NB + lead_spans) // spans_here
    before = neigh_ids[None, :] < neigh_ids[:, None]
    same_owner = owner_row[None, :] == owner_row[:, None]
    same_dest = dest_dev[None, :] == dest_dev[:, None]
    slot_of = jnp.sum(before & same_owner, axis=1)
    pair_rank = jnp.sum(before & same_owner & same_dest, axis=1)
    target = dest_dev * PAIR_CAP + pair_rank
    place_ids = jnp.arange(seq_count * PAIR_CAP, dtype=jnp.int32)
    is_mine = (owner_row == seq_index) & (dest_dev < seq_count)
    hit_map = (target[None, :] == place_ids[:, None]) & is_mine[None, :]
    slot_at = jnp.sum(jnp.where(hit_map, slot_of[None, :], 0), axis=1)
    slot_at_ok = jnp.any(hit_map, axis=1)
    slot_ids = jnp.arange(enc_cap, dtype=jnp.int32)
    owned_map = (slot_of[None, :] == slot_ids[:, None]) & is_mine[None, :]
    place_of_slot = jnp.sum(jnp.where(owned_map, target[None, :], 0), axis=1)
    place_ok = jnp.any(owned_map, axis=1)
    local_rows = NB * spans_here
    local_ids = jnp.arange(local_rows, dtype=jnp.int32)
    wanted = seq_index * local_rows - lead_spans * NB + local_ids
    arrive_ok = wanted >= 0
    safe_ids = jnp.maximum(wanted, 0)
    arrive_at = jnp.take(owner_row, safe_ids) * PAIR_CAP + jnp.take(pair_rank, safe_ids)
    landing = (arrive_at[None, :] == place_ids[:, None]) & arrive_ok[None, :]
    local_at = jnp.sum(jnp.where(landing, local_ids[None, :], 0), axis=1)
    local_ok = jnp.any(landing, axis=1)
    return (slot_at, slot_at_ok, place_of_slot, place_ok, arrive_at, arrive_ok, local_at, local_ok)


def block_step(query_blk, key_blk, value_blk, grad_blk, sink, is_live):
    scores = jnp.einsum(
        "cqhd,ckhd->chqk", query_blk, key_blk, preferred_element_type=jnp.float32
    ) * HD ** (-0.5)
    floor_logit = jnp.broadcast_to(sink[None, :, None], scores.shape[:3])
    live_rows = is_live[:, None, None]
    largest = jnp.where(live_rows, jnp.maximum(jnp.max(scores, axis=-1), floor_logit), floor_logit)
    powers = jnp.where(live_rows[..., None], jnp.exp(scores - largest[..., None]), 0.0)
    totals = jnp.exp(floor_logit - largest) + jnp.sum(powers, axis=-1)
    weights = powers / totals[..., None]
    low_weights = weights.astype(jnp.bfloat16)
    context = jnp.einsum(
        "chqk,ckhd->cqhd", low_weights, value_blk, preferred_element_type=jnp.float32
    )
    d_weights = jnp.einsum(
        "cqhd,ckhd->chqk", grad_blk, value_blk, preferred_element_type=jnp.float32
    )
    deltas = jnp.einsum("cqhd,cqhd->chq", grad_blk.astype(jnp.float32), context)
    d_scores = (weights * (d_weights - deltas[..., None]) * HD ** (-0.5)).astype(jnp.bfloat16)
    grad_query = jnp.einsum(
        "chqk,ckhd->cqhd", d_scores, key_blk, preferred_element_type=jnp.float32
    )
    grad_key = jnp.einsum(
        "chqk,cqhd->ckhd", d_scores, query_blk, preferred_element_type=jnp.float32
    )
    grad_value = jnp.einsum(
        "chqk,cqhd->ckhd", low_weights, grad_blk, preferred_element_type=jnp.float32
    )
    sink_part = -jnp.sum(jnp.exp(floor_logit - largest) / totals * deltas, axis=(0, 2))
    return (
        context.astype(jnp.bfloat16),
        grad_query.astype(jnp.bfloat16),
        grad_key.astype(jnp.bfloat16),
        grad_value.astype(jnp.bfloat16),
        sink_part,
    )


def move_encodings(enc_slots, owner_row, seq_index, seq_count, query_blk, grad_blk, sink, is_live):
    spans_here = query_blk.shape[0]
    local_heads = query_blk.shape[2]
    local_width = local_heads * HD
    enc_cap = enc_slots.shape[1]
    nothing = jnp.zeros((), enc_slots.dtype)
    lead_spans = 0
    slot_at, slot_at_ok, place_of_slot, place_ok, arrive_at, arrive_ok, local_at, local_ok = (
        routing(owner_row, seq_index, seq_count, spans_here, enc_cap, lead_spans)
    )
    outgoing = jnp.where(
        slot_at_ok[None, :, None, None], jnp.take(enc_slots, slot_at, axis=1), nothing
    )
    arrived = lax.all_to_all(outgoing, "seq", split_axis=1, concat_axis=1, tiled=True)
    nearby = jnp.where(
        arrive_ok[None, :, None, None], jnp.take(arrived, arrive_at, axis=1), nothing
    )
    carried = from_behind(nearby[:, -NB:], "seq", 1)
    nearby = jnp.concatenate([carried, nearby[:, :-NB]], axis=1)
    key_blk = nearby[0].reshape(spans_here, NB * NL, local_heads, HD)
    value_blk = nearby[1].reshape(spans_here, NB * NL, local_heads, HD)
    attended, grad_query, grad_key, grad_value, sink_part = block_step(
        query_blk, key_blk, value_blk, grad_blk, sink, is_live
    )
    neigh_grads = jnp.stack(
        [
            grad_key.reshape(NB * spans_here, NL, local_width),
            grad_value.reshape(NB * spans_here, NL, local_width),
        ]
    )
    returned_edge = from_behind(neigh_grads[:, :NB], "seq", -1)
    neigh_grads = jnp.concatenate([neigh_grads[:, NB:], returned_edge], axis=1)
    outbound = jnp.where(
        local_ok[None, :, None, None], jnp.take(neigh_grads, local_at, axis=1), nothing
    )
    inbound = lax.all_to_all(outbound, "seq", split_axis=1, concat_axis=1, tiled=True)
    enc_grads = jnp.where(
        place_ok[None, :, None, None], jnp.take(inbound, place_of_slot, axis=1), nothing
    )
    return (attended, grad_query, enc_grads, sink_part)


def on_device(queries, encodings, sink, owner, doc_start, d_out):
    seq_count = lax.axis_size("seq")
    seq_index = lax.axis_index("seq")
    query_rows = queries[0]
    grad_rows = d_out[0]
    enc_slots = encodings[0]
    owner_row = owner[0]
    tokens_here, local_width = query_rows.shape
    spans_here = tokens_here // CH
    local_heads = local_width // HD
    first_span = seq_index * spans_here
    span_ids = first_span + jnp.arange(spans_here, dtype=jnp.int32)
    doc_here = lax.dynamic_slice_in_dim(doc_start[0], first_span, spans_here)
    is_live = (span_ids >= 1) & (doc_here == 0)
    query_blk = query_rows.reshape(spans_here, CH, local_heads, HD)
    grad_blk = grad_rows.reshape(spans_here, CH, local_heads, HD)
    results = move_encodings(
        enc_slots, owner_row, seq_index, seq_count, query_blk, grad_blk, sink, is_live
    )
    attended, grad_query, enc_grads, sink_part = results
    sink_total = lax.psum(sink_part, ("seq", "dp"))
    return (
        attended.reshape(1, tokens_here, local_width),
        grad_query.reshape(1, tokens_here, local_width),
        enc_grads[None],
        sink_total,
    )


def solution(mesh):
    in_specs = (
        P("dp", "seq", "mp"),
        P("dp", None, "seq", None, "mp"),
        P("mp"),
        P("dp", None),
        P("dp", None),
        P("dp", "seq", "mp"),
    )
    out_specs = (
        P("dp", "seq", "mp"),
        P("dp", "seq", "mp"),
        P("dp", None, "seq", None, "mp"),
        P("mp"),
    )
    return jax.shard_map(
        on_device, mesh=mesh, in_specs=in_specs, out_specs=out_specs, check_vma=False
    )
```

profile of v0, /device:TPU:1, one launch (start us, length us, event | category | flops | bytes accessed | tf_op | source)
XLA Modules:
  0.0 409.6 jit_solution(2472035680862193637)
XLA Ops:
  1.3 0.9 convert_reduce_fusion.1
  2.5 7.0 %gather_fusion = bf16[32,2,128,512]{3,2,1,0:T(8,128)(2,1)} fusion(bf16[2,16,128,512]{3,2,1,0:T(8,128)(2,1)} %bitcast.64, s32[1024]{0:T(1024)S(1)} %get-tuple-element.27), kind=kCustom, calls=%fused_computation.2 | custom fusion | bytes 16777344 | tf_op jit(solution)/shard_map/jit(_take)/gather | solution.py:99
  9.5 7.6 %select_bitcast_fusion.1 = bf16[2,32,128,512]{3,2,0,1:T(8,128)(2,1)} fusion(bf16[32,2,128,512]{3,2,1,0:T(8,128)(2,1)} %gather_fusion, pred[32]{0:T(512)(128)(4,1)S(1)} %fusion.25, pred[32]{0:T(512)(128)(4,1)S(1)} %compare_and_fusion.2), kind=kLoop, calls=%fused_computation.7 | loop fusion | flops 8388608 | bytes 16777280 | tf_op jit(solution)/shard_map/jit(_where)/select_n | solution.py:98
  17.1 7.8 %all-to-all-start = ((bf16[2,32,128,512]{3,2,0,1:T(8,128)(2,1)}), bf16[2,32,128,512]{3,2,0,1:T(8,128)(2,1)}, u32[]{:S(2)}, u32[]{:S(2)}) async-start(bf16[2,32,128,512]{3,2,0,1:T(8,128)(2,1)} %select_bitcast_fusion.1), calls=%async_computation | async-start | bytes 16777216 | tf_op jit(solution)/shard_map/all_to_all | solution.py:101
  26.2 121.8 %all-to-all-done = bf16[2,32,128,512]{3,2,0,1:T(8,128)(2,1)} async-done(((bf16[2,32,128,512]{3,2,0,1:T(8,128)(2,1)}), bf16[2,32,128,512]{3,2,0,1:T(8,128)(2,1)}, u32[]{:S(2)}, u32[]{:S(2)}) %all-to-all-start) | async-done | bytes 8388640 | tf_op jit(solution)/shard_map/all_to_all | solution.py:101
  148.1 5.4 %gather_fusion.1 = bf16[8,2,128,512]{3,2,1,0:T(8,128)(2,1)} fusion(bf16[2,32,128,512]{3,2,0,1:T(8,128)(2,1)} %all-to-all-done, s32[1024]{0:T(1024)S(1)} %pad_clamp_fusion.2), kind=kCustom, calls=%fused_computation.3 | custom fusion | bytes 4194336 | tf_op jit(solution)/shard_map/jit(_take)/gather | solution.py:103
  153.5 1.9 select_bitcast_fusion.2
  155.4 1.3 collective-permute-start
  156.8 0.8 reshape_squeeze.15
  157.5 1.0 reshape_squeeze.14
  158.9 7.5 %collective-permute-done = bf16[2,2,128,512]{3,2,0,1:T(8,128)(2,1)S(1)} collective-permute-done((bf16[2,2,128,512]{3,2,0,1:T(8,128)(2,1)S(1)}, bf16[2,2,128,512]{3,2,0,1:T(8,128)(2,1)S(1)}, u32[]{:S(2)}, u32[]{:S(2)}) %collective-permute-start) | collective-permute-done | bytes 524320 | tf_op jit(solution)/shard_map/ppermute | solution.py:16
  166.9 1.1 reshape_squeeze.12
  169.2 2.4 bitcast_convert_fusion
  171.6 1.9 fusion.2
  174.1 2.7 fusion.7
  176.8 0.8 copy.52
  178.0 1.5 fusion.1
  179.6 0.8 copy.50
  180.4 1.2 stack_reshape.6
  181.6 1.3 constant_dynamic-update-slice_fusion.1
  183.0 1.5 collective-permute-start.1
  184.8 12.1 %collective-permute-done.1 = bf16[2,2,128,512]{3,2,1,0:T(8,128)(2,1)S(1)} collective-permute-done((bf16[2,2,128,512]{3,2,1,0:T(8,128)(2,1)S(1)}, bf16[2,2,128,512]{3,2,1,0:T(8,128)(2,1)S(1)}, u32[]{:S(2)}, u32[]{:S(2)}) %collective-permute-start.1) | collective-permute-done | bytes 524320 | tf_op jit(solution)/shard_map/ppermute | solution.py:16
  197.1 4.8 %gather_fusion.2 = bf16[32,2,128,512]{3,2,1,0:T(8,128)(2,1)} fusion(bf16[2,8,128,512]{3,2,1,0:T(8,128)(2,1)S(1)} %pad_maximum_fusion, s32[1024]{0:T(1024)S(1)} %pad_clamp_fusion.1), kind=kCustom, calls=%fused_computation.4 | custom fusion | bytes 16777344 | tf_op jit(solution)/shard_map/jit(_take)/gather | solution.py:121
  201.9 7.6 %select_bitcast_fusion = bf16[2,32,128,512]{3,2,0,1:T(8,128)(2,1)} fusion(bf16[32,2,128,512]{3,2,1,0:T(8,128)(2,1)} %gather_fusion.2, pred[32]{0:T(512)(128)(4,1)S(1)} %fusion.30, pred[32]{0:T(512)(128)(4,1)S(1)} %compare_and_fusion), kind=kLoop, calls=%fused_computation.6 | loop fusion | flops 8388608 | bytes 16777280 | tf_op jit(solution)/shard_map/jit(_where)/select_n | solution.py:120
  209.5 8.9 %all-to-all-start.1 = ((bf16[2,32,128,512]{3,2,0,1:T(8,128)(2,1)}), bf16[2,32,128,512]{3,2,0,1:T(8,128)(2,1)}, u32[]{:S(2)}, u32[]{:S(2)}) async-start(bf16[2,32,128,512]{3,2,0,1:T(8,128)(2,1)} %select_bitcast_fusion), calls=%async_computation.1 | async-start | bytes 16777216 | tf_op jit(solution)/shard_map/all_to_all | solution.py:123
  218.9 169.3 %psum.7 = f32[4]{0:T(128)} all-reduce(f32[4]{0:T(128)S(1)} %neg.3), channel_id=1, replica_groups=mesh['seq'=16,'mp'=8,'dp'=2] {'seq','dp'}, use_global_device_ids=true, to_apply=%region_11.13 | all-reduce | flops 4 | bytes 32 | tf_op jit(solution)/shard_map/psum | solution.py:150
  388.4 0.8 reshape.260
  389.8 0.8 reshape.261
  390.6 7.6 %copy.53 = bf16[2,32,128,512]{3,2,1,0:T(8,128)(2,1)} copy(bf16[2,32,128,512]{3,2,0,1:T(8,128)(2,1)} %all-to-all-done.1) | data formatting | bytes 16777216 | tf_op jit(solution)/shard_map/all_to_all | solution.py:123
  398.1 6.2 %gather_fusion.3 = bf16[16,2,128,512]{3,2,1,0:T(8,128)(2,1)} fusion(bf16[2,32,128,512]{3,2,1,0:T(8,128)(2,1)} %copy.53, s32[1024]{0:T(1024)S(1)} %pad_clamp_fusion), kind=kCustom, calls=%fused_computation.5 | custom fusion | bytes 8388672 | tf_op jit(solution)/shard_map/jit(_take)/gather | solution.py:125
  404.4 2.7 fusion
  407.1 2.5 copy.54
  (63 shorter events, 7.0 us)
Async XLA Ops:
  17.1 8.4 %copy-start = (s32[1,128]{1,0:T(1,128)S(1)}, s32[1,128]{1,0:T(1,128)}, u32[]{:S(2)}) copy-start(s32[1,128]{1,0:T(1,128)} %param.11) | copy-start | bytes 1540
  17.1 131.0 %all-to-all-start = ((bf16[2,32,128,512]{3,2,0,1:T(8,128)(2,1)}), bf16[2,32,128,512]{3,2,0,1:T(8,128)(2,1)}, u32[]{:S(2)}, u32[]{:S(2)}) async-start(bf16[2,32,128,512]{3,2,0,1:T(8,128)(2,1)} %select_bitcast_fusion.1), calls=%async_computation | async-start | bytes 16777216 | tf_op jit(solution)/shard_map/all_to_all | solution.py:101
  26.2 130.5 %copy-start.4 = (bf16[1,256,512]{2,1,0:T(8,128)(2,1)S(1)}, bf16[1,256,512]{2,1,0:T(8,128)(2,1)}, u32[]{:S(2)}) copy-start(bf16[1,256,512]{2,1,0:T(8,128)(2,1)} %param.13) | copy-start | bytes 786436
  153.5 5.1 %copy-start.7 = (s32[1,64]{1,0:T(1,128)S(1)}, s32[1,64]{1,0:T(1,128)}, u32[]{:S(2)}) copy-start(s32[1,64]{1,0:T(1,128)} %param.12) | copy-start | bytes 772
  155.4 11.0 %collective-permute-start = (bf16[2,2,128,512]{3,2,0,1:T(8,128)(2,1)S(1)}, bf16[2,2,128,512]{3,2,0,1:T(8,128)(2,1)S(1)}, u32[]{:S(2)}, u32[]{:S(2)}) collective-permute-start(bf16[2,2,128,512]{3,2,0,1:T(8,128)(2,1)S(1)} %slice.36), channel_id=1, source_target_pairs={{0,16},{16,32},{32,48},{48,64},{64,80},{80,96},{96,112},{112,128},... | collective-permute-start | bytes 1572872 | tf_op jit(solution)/shard_map/ppermute | solution.py:16
  166.6 2.0 copy-start.6
  168.5 3.1 copy-start.2
  174.1 2.7 copy-start.3
  183.0 13.9 %collective-permute-start.1 = (bf16[2,2,128,512]{3,2,1,0:T(8,128)(2,1)S(1)}, bf16[2,2,128,512]{3,2,1,0:T(8,128)(2,1)S(1)}, u32[]{:S(2)}, u32[]{:S(2)}) collective-permute-start(bf16[2,2,128,512]{3,2,1,0:T(8,128)(2,1)S(1)} %slice.41), channel_id=1, source_target_pairs={{16,0},{32,16},{48,32},{64,48},{80,64},{96,80},{112,96},{128,112},... | collective-permute-start | bytes 1572872 | tf_op jit(solution)/shard_map/ppermute | solution.py:16
  209.5 178.7 %copy-start.5 = (bf16[4,64,4,128]{3,1,2,0:T(8,128)(2,1)S(1)}, bf16[4,64,4,128]{3,1,2,0:T(8,128)(2,1)}, u32[]{:S(2)}) copy-start(bf16[4,64,4,128]{3,1,2,0:T(8,128)(2,1)} %get-tuple-element.25) | copy-start | bytes 786436
  209.5 179.7 %copy-start.1 = (bf16[4,4,64,256]{3,2,1,0:T(8,128)(2,1)S(1)}, bf16[4,4,64,256]{3,2,1,0:T(8,128)(2,1)}, u32[]{:S(2)}) copy-start(bf16[4,4,64,256]{3,2,1,0:T(8,128)(2,1)} %fusion.7) | copy-start | bytes 1572868
  209.5 181.1 %all-to-all-start.1 = ((bf16[2,32,128,512]{3,2,0,1:T(8,128)(2,1)}), bf16[2,32,128,512]{3,2,0,1:T(8,128)(2,1)}, u32[]{:S(2)}, u32[]{:S(2)}) async-start(bf16[2,32,128,512]{3,2,0,1:T(8,128)(2,1)} %select_bitcast_fusion), calls=%async_computation.1 | async-start | bytes 16777216 | tf_op jit(solution)/shard_map/all_to_all | solution.py:123
where the time goes:
time: 415 us; the launch traced here: 410 us
  blocking collectives  169 us (41%)
  waiting for transfers between devices  141 us (34%)
  local copies, waits for them, and re-layouts  45.1 us (11%)
  other arithmetic  23.8 us (6%)
  starting transfers between devices  19.5 us (5%)
  matrix products  9.42 us (2%)
    psum x1, blocking collectives, on_device(): sink_total = lax.psum(sink_part, ('seq', 'dp'))  169 us
    all_to_all x1, waiting for transfers between devices, move_encodings(): lax.all_to_all(outgoing, 'seq', split_axis=1, concat_axis=1, tiled=True)  122 us
    ppermute x2, waiting for transfers between devices, from_behind(): return lax.ppermute(block, axis, route)  19.6 us
    all_to_all x1, starting transfers between devices, move_encodings(): lax.all_to_all(outbound, 'seq', split_axis=1, concat_axis=1, tiled=True)  8.9 us
  transfers between devices with their start and end apart: 4, of which 3 were waited for; matrix products, arithmetic and copies ran while one was open for 2% of the time, Pallas kernels for 0%

commit v1 on v0

v1 whole, which is shorter than its diff:
```python
import functools

import jax
import jax.numpy as jnp
from jax import lax
from jax.experimental import pallas as pl
from jax.experimental.pallas import tpu as pltpu
from jax.sharding import PartitionSpec as P

HD = 128
CH = 64
NB = 2
NL = 128
HALF = CH // 2
SCALE = HD ** (-0.5)
VMEM = 56 * 1024 * 1024
SLOT_STEP = 4


def params():
    return pltpu.CompilerParams(vmem_limit_bytes=VMEM)


def cost(flops, data):
    return pl.CostEstimate(flops=flops, bytes_accessed=data, transcendentals=0)


def cut_stripes(query_ref, grad_ref, out_ref):
    spans, heads = out_ref.shape[1], query_ref.shape[1] // HD
    for which, ref in enumerate((query_ref, grad_ref)):
        for head in range(heads):
            for half in range(2):
                stripe = (which * heads + head) * 2 + half
                for span in range(spans):
                    row = span * CH + half * HALF
                    out_ref[stripe, span] = ref[row : row + HALF, head * HD : (head + 1) * HD]


def join_stripes(in_ref, attended_ref, query_ref):
    spans, heads = in_ref.shape[1], attended_ref.shape[1] // HD
    for which, ref in enumerate((attended_ref, query_ref)):
        for head in range(heads):
            for half in range(2):
                stripe = (which * heads + head) * 2 + half
                for span in range(spans):
                    row = span * CH + half * HALF
                    ref[row : row + HALF, head * HD : (head + 1) * HD] = in_ref[stripe, span]


def spread_spans(meta_ref, in_ref, out_ref):
    count = out_ref.shape[0]
    first = pl.program_id(0) * count

    def body(i, carry):
        out_ref[i] = in_ref[meta_ref[first + i] & 63]
        return carry

    lax.fori_loop(0, count, body, 0, unroll=8)


def add_partials(meta_ref, in_ref, out_ref, *, pos_at):
    def body(span, carry):
        here = pos_at + 2 * span - NB
        left = in_ref[meta_ref[here]].astype(jnp.float32)
        right = in_ref[meta_ref[here + 1]].astype(jnp.float32)
        out_ref[span] = (left + right).astype(jnp.bfloat16)
        return carry

    out_ref[0] = jnp.zeros(out_ref.shape[1:], jnp.bfloat16)
    lax.fori_loop(1, out_ref.shape[0], body, 0, unroll=7)


def paired(stripes_ref, which, pair, slot, heads):
    nothing = jnp.zeros((CH, HD), jnp.bfloat16)
    blocks = []
    for head in (2 * pair, 2 * pair + 1):
        at = (which * heads + head) * 2
        blocks.append(jnp.concatenate([stripes_ref[at, slot], stripes_ref[at + 1, slot]], axis=0))
    return jnp.concatenate(
        [
            jnp.concatenate([blocks[0], nothing], axis=1),
            jnp.concatenate([nothing, blocks[1]], axis=1),
        ],
        axis=0,
    )


def dot(left, right, left_dim, right_dim):
    return lax.dot_general(
        left, right, (((left_dim,), (right_dim,)), ((), ())), preferred_element_type=jnp.float32
    )


def stats_of(stripes_ref, enc_ref, out_ref):
    heads = enc_ref.shape[3] // HD
    pairs = heads // 2
    for slot in range(enc_ref.shape[1]):
        for pair in range(pairs):
            cols = slice(pair * 2 * HD, (pair + 1) * 2 * HD)
            queries = paired(stripes_ref, 0, pair, slot, heads)
            grads = paired(stripes_ref, 1, pair, slot, heads)
            scores = dot(enc_ref[0, slot, :, cols], queries, 1, 1) * SCALE
            d_weights = dot(enc_ref[1, slot, :, cols], grads, 1, 1)
            top = jnp.max(scores, axis=0, keepdims=True)
            powers = jnp.exp(scores - top)
            total = jnp.sum(powers, axis=0, keepdims=True)
            delta = jnp.sum(powers * d_weights, axis=0, keepdims=True) / total
            log_total = top + jnp.log(total)
            for dest in range(out_ref.shape[0]):
                out_ref[dest, slot, pair : pair + 1] = log_total
                out_ref[dest, slot, pairs + pair : pairs + pair + 1] = delta


def joined(mine, other, sink):
    pairs = sink.shape[0]
    log_a, log_b = mine[:pairs], other[:pairs]
    top = jnp.maximum(jnp.maximum(log_a, log_b), sink)
    part_a, part_b, part_s = jnp.exp(log_a - top), jnp.exp(log_b - top), jnp.exp(sink - top)
    total = part_a + part_b + part_s
    deltas = (part_a * mine[pairs:] + part_b * other[pairs:]) / total
    return top + jnp.log(total), deltas, part_s / total


def slot_terms(meta_ref, stripes_ref, enc_ref, stats_ref, sink_ref, slot, me_at):
    heads = enc_ref.shape[3] // HD
    here = pl.program_id(0) * enc_ref.shape[1] + slot
    mine_at = meta_ref[me_at] + here
    code = meta_ref[mine_at]
    live = ((code >> 6) & 1).astype(jnp.float32)
    log_total, deltas, _ = joined(stats_ref[mine_at], stats_ref[code >> 7], sink_ref[...])
    for pair in range(heads // 2):
        cols = slice(pair * 2 * HD, (pair + 1) * 2 * HD)
        queries = paired(stripes_ref, 0, pair, slot, heads)
        grads = paired(stripes_ref, 1, pair, slot, heads)
        keys, values = enc_ref[0, slot, :, cols], enc_ref[1, slot, :, cols]
        scores = dot(keys, queries, 1, 1) * SCALE
        d_weights = dot(values, grads, 1, 1)
        weights = jnp.exp(scores - log_total[pair : pair + 1]) * live
        d_scores = (weights * (d_weights - deltas[pair : pair + 1]) * SCALE).astype(jnp.bfloat16)
        yield pair, cols, queries, grads, keys, values, weights.astype(jnp.bfloat16), d_scores


def token_side(meta_ref, stripes_ref, enc_ref, stats_ref, sink_ref, out_ref, *, me_at):
    heads = enc_ref.shape[3] // HD
    for slot in range(enc_ref.shape[1]):
        for pair, _, _, _, keys, values, weights, d_scores in slot_terms(
            meta_ref, stripes_ref, enc_ref, stats_ref, sink_ref, slot, me_at
        ):
            for which, (left, right) in enumerate(((weights, values), (d_scores, keys))):
                rows = dot(left, right, 0, 0).astype(jnp.bfloat16)
                for side in range(2):
                    for half in range(2):
                        stripe = (which * heads + 2 * pair + side) * 2 + half
                        at = side * CH + half * HALF
                        out_ref[stripe, slot] = rows[at : at + HALF, side * HD : (side + 1) * HD]


def slot_side(meta_ref, stripes_ref, enc_ref, stats_ref, sink_ref, out_ref, *, me_at):
    for slot in range(enc_ref.shape[1]):
        for _, cols, queries, grads, _, _, weights, d_scores in slot_terms(
            meta_ref, stripes_ref, enc_ref, stats_ref, sink_ref, slot, me_at
        ):
            out_ref[0, slot, :, cols] = dot(d_scores, queries, 1, 0).astype(jnp.bfloat16)
            out_ref[1, slot, :, cols] = dot(weights, grads, 1, 0).astype(jnp.bfloat16)


def sink_side(meta_ref, stats_ref, sink_ref, out_ref, *, pos_at, live_at, spans):
    sink = sink_ref[...]

    def body(span, total):
        here = pos_at + 2 * span - NB
        live = meta_ref[live_at + span].astype(jnp.float32)
        _, deltas, part = joined(stats_ref[meta_ref[here]], stats_ref[meta_ref[here + 1]], sink)
        return total - part * deltas * live

    out_ref[...] = lax.fori_loop(1, spans, body, jnp.zeros_like(sink), unroll=7)


def routing(owner_row, doc_row, seq_index, slots, seq_count):
    neigh_count, spans = owner_row.shape[0], doc_row.shape[0]
    neigh_ids = jnp.arange(neigh_count, dtype=jnp.int32)
    before = neigh_ids[None, :] < neigh_ids[:, None]
    same_owner = owner_row[None, :] == owner_row[:, None]
    slot_of = jnp.sum(before & same_owner, axis=1).astype(jnp.int32)
    place = owner_row * slots + slot_of
    other = jnp.flip(place.reshape(spans, NB), axis=1).reshape(-1)
    span_ids = jnp.arange(spans, dtype=jnp.int32)
    live = ((span_ids >= 1) & (doc_row == 0)).astype(jnp.int32)
    next_live = jnp.concatenate([live[1:], jnp.zeros((1,), jnp.int32)])
    reader = jnp.minimum(neigh_ids // NB + 1, spans - 1)
    code = reader + 64 * jnp.repeat(next_live, NB) + 128 * other
    flat = jnp.arange(slots * seq_count, dtype=jnp.int32)
    codes = jnp.sum(jnp.where(place[None, :] == flat[:, None], code[None, :], 0), axis=1)
    first = (seq_index * slots).astype(jnp.int32).reshape(1)
    return jnp.concatenate([codes, place, live, first])


def on_device(queries, encodings, sink, owner, doc_start, d_out):
    seq_count = lax.axis_size("seq")
    seq_index = lax.axis_index("seq")
    tokens, width = queries.shape[1:]
    spans_here = tokens // CH
    heads = width // HD
    pairs = heads // 2
    slots = encodings.shape[2]
    spans, neighs = doc_start.shape[1], owner.shape[1]
    places = seq_count * slots
    pos_at = places
    live_at = pos_at + neighs
    me_at = live_at + spans
    bf16 = jnp.bfloat16
    f32 = jnp.float32

    meta = routing(owner[0], doc_start[0], seq_index, slots, seq_count)
    sink_rows = jnp.repeat(sink.reshape(pairs, 2), CH, axis=1)

    def everywhere(block):
        return lax.all_to_all(block, "seq", split_axis=0, concat_axis=0, tiled=True)

    stripe = (HALF, HD)
    cut = pl.pallas_call(
        cut_stripes,
        out_shape=jax.ShapeDtypeStruct((seq_count, spans_here) + stripe, bf16),
        compiler_params=params(),
        name="cut_stripes",
    )(queries[0], d_out[0])
    all_spans = everywhere(cut).reshape((spans,) + stripe)

    per = places // 4
    spread = pl.pallas_call(
        spread_spans,
        grid_spec=pltpu.PrefetchScalarGridSpec(
            num_scalar_prefetch=1,
            grid=(4,),
            in_specs=[pl.BlockSpec((spans,) + stripe, lambda i, m: (0, 0, 0))],
            out_specs=pl.BlockSpec((per,) + stripe, lambda i, m: (i, 0, 0)),
        ),
        out_shape=jax.ShapeDtypeStruct((places,) + stripe, bf16),
        compiler_params=params(),
        name="spread_spans",
    )(meta, all_spans)
    stripes = everywhere(spread.reshape((seq_count, slots) + stripe))

    enc = encodings[0]
    grid = (slots // SLOT_STEP,)
    stripes_block = (seq_count, SLOT_STEP) + stripe
    enc_block = (2, SLOT_STEP, NL, width)
    one_dot = 2 * NL * CH * width * slots
    stats = pl.pallas_call(
        stats_of,
        grid=grid,
        in_specs=[
            pl.BlockSpec(stripes_block, lambda i: (0, i, 0, 0)),
            pl.BlockSpec(enc_block, lambda i: (0, i, 0, 0)),
        ],
        out_specs=pl.BlockSpec((seq_count, SLOT_STEP, heads, HD), lambda i: (0, i, 0, 0)),
        out_shape=jax.ShapeDtypeStruct((seq_count, slots, heads, HD), f32),
        compiler_params=params(),
        cost_estimate=cost(2 * one_dot, stripes.size * 2 + enc.size * 2),
        name="stats",
    )(stripes, enc)
    all_stats = everywhere(stats).reshape(places, heads, HD)

    def with_stats(kernel, out_block, out_shape, name):
        return pl.pallas_call(
            functools.partial(kernel, me_at=me_at),
            grid_spec=pltpu.PrefetchScalarGridSpec(
                num_scalar_prefetch=1,
                grid=grid,
                in_specs=[
                    pl.BlockSpec(stripes_block, lambda i, m: (0, i, 0, 0)),
                    pl.BlockSpec(enc_block, lambda i, m: (0, i, 0, 0)),
                    pl.BlockSpec((places, heads, HD), lambda i, m: (0, 0, 0)),
                    pl.BlockSpec((pairs, HD), lambda i, m: (0, 0)),
                ],
                out_specs=pl.BlockSpec(out_block, lambda i, m: (0, i, 0, 0)),
            ),
            out_shape=jax.ShapeDtypeStruct(out_shape, bf16),
            compiler_params=params(),
            cost_estimate=cost(4 * one_dot, stripes.size * 2 + enc.size * 4),
            name=name,
        )(meta, stripes, enc, all_stats, sink_rows)

    partials = with_stats(token_side, stripes_block, stripes.shape, "token_side")
    returned = everywhere(partials).reshape((places,) + stripe)
    enc_grads = with_stats(slot_side, enc_block, enc.shape, "slot_side")

    sink_lanes = pl.pallas_call(
        functools.partial(sink_side, pos_at=pos_at, live_at=live_at, spans=spans),
        grid_spec=pltpu.PrefetchScalarGridSpec(
            num_scalar_prefetch=1,
            grid=(1,),
            in_specs=[
                pl.BlockSpec((places, heads, HD), lambda i, m: (0, 0, 0)),
                pl.BlockSpec((pairs, HD), lambda i, m: (0, 0)),
            ],
            out_specs=pl.BlockSpec((pairs, HD), lambda i, m: (0, 0)),
        ),
        out_shape=jax.ShapeDtypeStruct((pairs, HD), f32),
        compiler_params=params(),
        cost_estimate=cost(spans * 4096, all_stats.size * 4),
        name="sink_side",
    )(meta, all_stats, sink_rows)
    sink_part = jnp.sum(sink_lanes.reshape(heads, CH), axis=1)
    sink_total = sink_part + lax.ppermute(sink_part, "dp", [(0, 1), (1, 0)])

    summed = pl.pallas_call(
        functools.partial(add_partials, pos_at=pos_at),
        grid_spec=pltpu.PrefetchScalarGridSpec(
            num_scalar_prefetch=1,
            grid=(1,),
            in_specs=[pl.BlockSpec((places,) + stripe, lambda i, m: (0, 0, 0))],
            out_specs=pl.BlockSpec((spans,) + stripe, lambda i, m: (0, 0, 0)),
        ),
        out_shape=jax.ShapeDtypeStruct((spans,) + stripe, bf16),
        compiler_params=params(),
        name="add_partials",
    )(meta, returned)
    final = everywhere(summed.reshape((seq_count, spans_here) + stripe))
    attended, grad_query = pl.pallas_call(
        join_stripes,
        out_shape=[jax.ShapeDtypeStruct((tokens, width), bf16)] * 2,
        compiler_params=params(),
        name="join_stripes",
    )(final)
    return attended[None], grad_query[None], enc_grads[None], sink_total


def solution(mesh):
    in_specs = (
        P("dp", "seq", "mp"),
        P("dp", None, "seq", None, "mp"),
        P("mp"),
        P("dp", None),
        P("dp", None),
        P("dp", "seq", "mp"),
    )
    out_specs = (
        P("dp", "seq", "mp"),
        P("dp", "seq", "mp"),
        P("dp", None, "seq", None, "mp"),
        P("mp"),
    )
    return jax.shard_map(
        on_device, mesh=mesh, in_specs=in_specs, out_specs=out_specs, check_vma=False
    )
```

time: 415 us -> 145 us (0.35); the launches traced: 410 us -> 144 us
  waiting for transfers between devices: 141 us -> 16.8 us
  blocking collectives: 169 us -> 60.3 us
  Pallas kernels: 0 us -> 40.5 us
  local copies, waits for them, and re-layouts: 45.1 us -> 4.72 us
  other arithmetic: 23.8 us -> 1.7 us
  matrix products: 9.42 us -> 0 us
    psum x1 -> x0, blocking collectives: 169 us -> none  [on_device(): sink_total = lax.psum(sink_part, ('seq', 'dp'))]
    all_to_all x2 -> x3, waiting for transfers between devices: 122 us -> 16.8 us  [everywhere(): return lax.all_to_all(block, 'seq', split_axis=0, concat_axis=0, tiled=True)]
    all_to_all x0 -> x2, blocking collectives: none -> 60.3 us  [everywhere(): return lax.all_to_all(block, 'seq', split_axis=0, concat_axis=0, tiled=True)]
    pallas_call x0 -> x8, Pallas kernels: none -> 40.5 us  [the longest x2 21.7 us: with_stats(): pl.pallas_call(functools.partial(kernel, me_at=me_at), grid_spec=pltpu.Pr...]
    gather x6 -> x0, local copies, waits for them, and re-layouts: 24.7 us -> none  [the longest x1 6.97 us: move_encodings(): jnp.take(enc_slots, slot_at, axis=1)]
    select_n x10 -> x0, other arithmetic: 19.9 us -> none  [the longest x1 7.57 us: move_encodings(): jnp.where(local_ok[None, :, None, None], jnp.take(neigh_grads, local_at,...]
    ppermute x2 -> x1, waiting for transfers between devices: 19.6 us -> 0.01 us  [on_device(): sink_total = sink_part + lax.ppermute(sink_part, 'dp', [(0, 1), (1, 0)])]
    dot_general x6 -> x0, matrix products: 9.42 us -> none  [the longest x1 2.7 us: block_step(): jnp.einsum('cqhd,ckhd->chqk', grad_blk, value_blk, preferred_element_type...]
  transfers between devices with their start and end apart: 4 -> 4, of which waited for: 3 -> 2; matrix products, arithmetic and copies ran while one was open for 2% -> 3% of each run, Pallas kernels for 0% -> 9%
where the time goes in v1:
time: 145 us; the launch traced here: 144 us
  blocking collectives  60.3 us (42%)
  Pallas kernels  40.5 us (28%)
  starting transfers between devices  19.6 us (14%)
  waiting for transfers between devices  16.8 us (12%)
  local copies, waits for them, and re-layouts  4.72 us (3%)
  other arithmetic  1.7 us (1%)
    all_to_all x2, blocking collectives, everywhere(): return lax.all_to_all(block, 'seq', split_axis=0, concat_axis=0, tiled=True)  60.3 us
    pallas_call x2, Pallas kernels, with_stats(): pl.pallas_call(functools.partial(kernel, me_at=me_at), grid_spec=pltpu.Pr...  21.7 us
    all_to_all x3, waiting for transfers between devices, everywhere(): return lax.all_to_all(block, 'seq', split_axis=0, concat_axis=0, tiled=True)  16.8 us
    all_to_all x3, starting transfers between devices, everywhere(): return lax.all_to_all(block, 'seq', split_axis=0, concat_axis=0, tiled=True)  14.7 us
    pallas_call x1, Pallas kernels, on_device(): pl.pallas_call(stats_of, grid=grid, in_specs=[pl.BlockSpec(stripes_block,...  5.22 us
    ppermute x1, starting transfers between devices, on_device(): sink_total = sink_part + lax.ppermute(sink_part, 'dp', [(0, 1), (1, 0)])  4.9 us
    pallas_call x1, Pallas kernels, on_device(): pl.pallas_call(spread_spans, grid_spec=pltpu.PrefetchScalarGridSpec(num_s...  3.74 us
    pallas_call x1, Pallas kernels, on_device(): pl.pallas_call(functools.partial(add_partials, pos_at=pos_at), grid_spec=...  3.3 us
  transfers between devices with their start and end apart: 4, of which 2 were waited for; matrix products, arithmetic and copies ran while one was open for 3% of the time, Pallas kernels for 9%

profile of v1, /device:TPU:1, one launch (start us, length us, event | category | flops | bytes accessed | tf_op | source)
XLA Modules:
  0.0 144.4 jit_solution(3699224322052610842)
XLA Ops:
  0.7 1.9 %cut_stripes.1 = bf16[16,4,32,128]{3,2,1,0:T(8,128)(2,1)} custom-call(bf16[256,512]{1,0:T(8,128)(2,1)} %bitcast.35, bf16[256,512]{1,0:T(8,128)(2,1)} %bitcast.36), custom_call_target="tpu_custom_call" | custom-call | tf_op jit(solution)/shard_map/cut_stripes/pallas_call | solution.py:221
  2.6 7.6 %all-to-all-start = ((bf16[16,4,32,128]{3,2,1,0:T(8,128)(2,1)}), bf16[16,4,32,128]{3,2,1,0:T(8,128)(2,1)S(1)}, u32[]{:S(2)}, u32[]{:S(2)}) async-start(bf16[16,4,32,128]{3,2,1,0:T(8,128)(2,1)} %cut_stripes.1), calls=%async_computation | async-start | bytes 1048576 | tf_op jit(solution)/shard_map/all_to_all | solution.py:218
  10.2 0.2 convert_reduce_fusion
  10.4 0.1 reduce_sum.33
  10.5 0.1 mul.50
  10.8 0.1 mul.53
  11.0 0.1 add_multiply_fusion
  11.1 0.1 mul.49
  11.3 0.1 select_reduce_fusion
  11.4 0.7 pad_add_fusion.meta_ref
  12.1 8.6 %all-to-all-done = bf16[16,4,32,128]{3,2,1,0:T(8,128)(2,1)S(1)} async-done(((bf16[16,4,32,128]{3,2,1,0:T(8,128)(2,1)}), bf16[16,4,32,128]{3,2,1,0:T(8,128)(2,1)S(1)}, u32[]{:S(2)}, u32[]{:S(2)}) %all-to-all-start) | async-done | bytes 524320 | tf_op jit(solution)/shard_map/all_to_all | solution.py:218
  20.7 0.8 copy-done.2
  21.5 3.7 %spread_spans.1 = bf16[256,32,128]{2,1,0:T(8,128)(2,1)} custom-call(s32[449]{0:T(512)} %pad_add_fusion.meta_ref, bf16[64,32,128]{2,1,0:T(8,128)(2,1)} %bitcast.33), custom_call_target="tpu_custom_call" | custom-call | tf_op jit(solution)/shard_map/spread_spans/pallas_call | solution.py:230
  25.2 31.3 %all_to_all.25.stripes_ref = bf16[16,16,32,128]{3,2,1,0:T(8,128)(2,1)} all-to-all(bf16[16,16,32,128]{3,2,1,0:T(8,128)(2,1)} %bitcast.27), channel_id=1, replica_groups=mesh['seq'=16,'mp'=8,'dp'=2] {'seq'}, dimensions={0} | all-to-all | bytes 4194304 | tf_op jit(solution)/shard_map/all_to_all | solution.py:218
  56.5 5.2 %stats.1 = f32[16,16,4,128]{3,2,1,0:T(4,128)} custom-call(bf16[16,16,32,128]{3,2,1,0:T(8,128)(2,1)} %all_to_all.25.stripes_ref, bf16[2,16,128,512]{3,2,1,0:T(8,128)(2,1)} %bitcast.24), custom_call_target="tpu_custom_call" | custom-call | flops 268435456 | bytes 6291456 | tf_op jit(solution)/shard_map/stats/pallas_call | solution.py:249
  61.7 3.6 %all-to-all-start.2 = ((f32[16,16,4,128]{3,2,1,0:T(4,128)}), f32[16,16,4,128]{3,2,1,0:T(4,128)S(1)}, u32[]{:S(2)}, u32[]{:S(2)}) async-start(f32[16,16,4,128]{3,2,1,0:T(4,128)} %stats.1), calls=%async_computation.2 | async-start | bytes 1048576 | tf_op jit(solution)/shard_map/all_to_all | solution.py:218
  65.3 0.1 reshape.81
  65.5 0.6 reshape.82.sink_ref
  66.1 8.2 %all-to-all-done.2 = f32[16,16,4,128]{3,2,1,0:T(4,128)S(1)} async-done(((f32[16,16,4,128]{3,2,1,0:T(4,128)}), f32[16,16,4,128]{3,2,1,0:T(4,128)S(1)}, u32[]{:S(2)}, u32[]{:S(2)}) %all-to-all-start.2) | async-done | bytes 524320 | tf_op jit(solution)/shard_map/all_to_all | solution.py:218
  74.3 0.8 copy-done
  75.1 11.8 %token_side.1 = bf16[16,16,32,128]{3,2,1,0:T(8,128)(2,1)} custom-call(s32[449]{0:T(512)} %pad_add_fusion.meta_ref, bf16[16,16,32,128]{3,2,1,0:T(8,128)(2,1)} %all_to_all.25.stripes_ref, bf16[2,16,128,512]{3,2,1,0:T(8,128)(2,1)} %bitcast.25, f32[256,4,128]{2,1,0:T(4,128)} %bitcast.29, f32[2,128]{1,0:T(2,128)} %reshape.82.sink_ref), custom_call_target="tpu_custom_call" | custom-call | flops 536870912 | bytes 10485760 | tf_op jit(solution)/shard_map/token_side/pallas_call | solution.py:265
  86.9 29.0 %all_to_all.26 = bf16[16,16,32,128]{3,2,1,0:T(8,128)(2,1)} all-to-all(bf16[16,16,32,128]{3,2,1,0:T(8,128)(2,1)} %token_side.1), channel_id=1, replica_groups=mesh['seq'=16,'mp'=8,'dp'=2] {'seq'}, dimensions={0} | all-to-all | bytes 4194304 | tf_op jit(solution)/shard_map/all_to_all | solution.py:218
  115.9 3.3 %add_partials.1 = bf16[64,32,128]{2,1,0:T(8,128)(2,1)} custom-call(s32[449]{0:T(512)} %pad_add_fusion.meta_ref, bf16[256,32,128]{2,1,0:T(8,128)(2,1)} %bitcast.28), custom_call_target="tpu_custom_call" | custom-call | tf_op jit(solution)/shard_map/add_partials/pallas_call | solution.py:307
  119.2 3.6 %all-to-all-start.4 = ((bf16[16,4,32,128]{3,2,1,0:T(8,128)(2,1)}), bf16[16,4,32,128]{3,2,1,0:T(8,128)(2,1)S(1)}, u32[]{:S(2)}, u32[]{:S(2)}) async-start(bf16[16,4,32,128]{3,2,1,0:T(8,128)(2,1)} %bitcast.34), calls=%async_computation.4 | async-start | bytes 1048576 | tf_op jit(solution)/shard_map/all_to_all | solution.py:218
  122.8 2.7 %sink_side.1 = f32[2,128]{1,0:T(2,128)} custom-call(s32[449]{0:T(512)} %pad_add_fusion.meta_ref, f32[256,4,128]{2,1,0:T(4,128)} %bitcast.30, f32[2,128]{1,0:T(2,128)} %reshape.82.sink_ref), custom_call_target="tpu_custom_call" | custom-call | flops 262144 | bytes 524288 | tf_op jit(solution)/shard_map/sink_side/pallas_call | solution.py:288
  125.5 0.8 reshape.85
  126.3 0.1 reduce_sum.35
  126.4 4.9 %collective-permute-start = (f32[4]{0:T(128)S(1)}, f32[4]{0:T(128)S(1)}, u32[]{:S(2)}, u32[]{:S(2)}) collective-permute-start(f32[4]{0:T(128)S(1)} %reduce_sum.35), channel_id=1, source_target_pairs={{0,1},{1,0},{2,3},{3,2},{4,5},{5,4},{6,7},{7,6},{8,9},{9,8},{10,11... | collective-permute-start | bytes 56 | tf_op jit(solution)/shard_map/ppermute | solution.py:305
  131.3 9.9 %slot_side.1 = bf16[2,16,128,512]{3,2,1,0:T(8,128)(2,1)} custom-call(s32[449]{0:T(512)} %pad_add_fusion.meta_ref, bf16[16,16,32,128]{3,2,1,0:T(8,128)(2,1)} %all_to_all.25.stripes_ref, bf16[2,16,128,512]{3,2,1,0:T(8,128)(2,1)} %bitcast.26, f32[256,4,128]{2,1,0:T(4,128)} %bitcast.31, f32[2,128]{1,0:T(2,128)} %reshape.82.sink_ref), custom_call_target="tpu_custom_call" | custom-call | flops 536870912 | bytes 10485760 | tf_op jit(solution)/shard_map/slot_side/pallas_call | solution.py:265
  141.1 0.5 add.45
  141.7 0.8 copy-done.1
  142.5 1.9 %join_stripes.1 = (bf16[256,512]{1,0:T(8,128)(2,1)}, bf16[256,512]{1,0:T(8,128)(2,1)}) custom-call(bf16[16,4,32,128]{3,2,1,0:T(8,128)(2,1)} %copy-done.1), custom_call_target="tpu_custom_call" | custom-call | tf_op jit(solution)/shard_map/join_stripes/pallas_call | solution.py:320
  (21 shorter events, 0.4 us)
Async XLA Ops:
  0.6 9.5 %copy-start.3 = (s32[1,128]{1,0:T(1,128)S(1)}, s32[1,128]{1,0:T(1,128)}, u32[]{:S(2)}) copy-start(s32[1,128]{1,0:T(1,128)} %param.9) | copy-start | bytes 1540
  0.6 9.9 %copy-start.4 = (s32[1,64]{1,0:T(1,128)S(1)}, s32[1,64]{1,0:T(1,128)}, u32[]{:S(2)}) copy-start(s32[1,64]{1,0:T(1,128)} %param.10) | copy-start | bytes 772
  2.6 18.1 %all-to-all-start = ((bf16[16,4,32,128]{3,2,1,0:T(8,128)(2,1)}), bf16[16,4,32,128]{3,2,1,0:T(8,128)(2,1)S(1)}, u32[]{:S(2)}, u32[]{:S(2)}) async-start(bf16[16,4,32,128]{3,2,1,0:T(8,128)(2,1)} %cut_stripes.1), calls=%async_computation | async-start | bytes 1048576 | tf_op jit(solution)/shard_map/all_to_all | solution.py:218
  20.7 0.8 copy-start.2
  56.5 8.8 %copy-start.5 = (f32[4]{0:T(128)S(1)}, f32[4]{0:T(128)}, u32[]{:S(2)}) copy-start(f32[4]{0:T(128)} %param.8) | copy-start | bytes 52
  61.7 12.6 %all-to-all-start.2 = ((f32[16,16,4,128]{3,2,1,0:T(4,128)}), f32[16,16,4,128]{3,2,1,0:T(4,128)S(1)}, u32[]{:S(2)}, u32[]{:S(2)}) async-start(f32[16,16,4,128]{3,2,1,0:T(4,128)} %stats.1), calls=%async_computation.2 | async-start | bytes 1048576 | tf_op jit(solution)/shard_map/all_to_all | solution.py:218
  74.3 0.8 copy-start
  119.2 22.4 %all-to-all-start.4 = ((bf16[16,4,32,128]{3,2,1,0:T(8,128)(2,1)}), bf16[16,4,32,128]{3,2,1,0:T(8,128)(2,1)S(1)}, u32[]{:S(2)}, u32[]{:S(2)}) async-start(bf16[16,4,32,128]{3,2,1,0:T(8,128)(2,1)} %bitcast.34), calls=%async_computation.4 | async-start | bytes 1048576 | tf_op jit(solution)/shard_map/all_to_all | solution.py:218
  126.4 14.8 %collective-permute-start = (f32[4]{0:T(128)S(1)}, f32[4]{0:T(128)S(1)}, u32[]{:S(2)}, u32[]{:S(2)}) collective-permute-start(f32[4]{0:T(128)S(1)} %reduce_sum.35), channel_id=1, source_target_pairs={{0,1},{1,0},{2,3},{3,2},{4,5},{5,4},{6,7},{7,6},{8,9},{9,8},{10,11... | collective-permute-start | bytes 56 | tf_op jit(solution)/shard_map/ppermute | solution.py:305
  141.7 0.8 copy-start.1

commit v2 on v1

v2 whole, which is shorter than its diff:
```python
import functools

import jax
import jax.numpy as jnp
from jax import lax
from jax.experimental import pallas as pl
from jax.experimental.pallas import tpu as pltpu
from jax.sharding import PartitionSpec as P

HD = 128
CH = 64
NB = 2
NL = 128
HALF = CH // 2
SCALE = HD ** (-0.5)
MIB = 1024 * 1024
GRAD_STEPS = 4
IN_VMEM = pl.BlockSpec(memory_space=pltpu.VMEM)
IN_SMEM = pl.BlockSpec(memory_space=pltpu.SMEM)


def cut_stripes(query_ref, grad_ref, out_ref):
    spans, heads = out_ref.shape[1], query_ref.shape[1] // HD
    for which, ref in enumerate((query_ref, grad_ref)):
        for head in range(heads):
            for half in range(2):
                stripe = (which * heads + head) * 2 + half
                for span in range(spans):
                    row = span * CH + half * HALF
                    out_ref[stripe, span] = ref[row : row + HALF, head * HD : (head + 1) * HD]


def join_stripes(in_ref, attended_ref, query_ref):
    spans, heads = in_ref.shape[1], attended_ref.shape[1] // HD
    for which, ref in enumerate((attended_ref, query_ref)):
        for head in range(heads):
            for half in range(2):
                stripe = (which * heads + head) * 2 + half
                for span in range(spans):
                    row = span * CH + half * HALF
                    ref[row : row + HALF, head * HD : (head + 1) * HD] = in_ref[stripe, span]


def spread_spans(meta_ref, in_ref, out_ref):
    def body(i, carry):
        out_ref[i] = in_ref[meta_ref[i] & 63]
        return carry

    lax.fori_loop(0, out_ref.shape[0], body, 0, unroll=16)


def add_partials(meta_ref, in_ref, out_ref, *, pos_at):
    def body(span, carry):
        here = pos_at + 2 * span - NB
        left = in_ref[meta_ref[here]].astype(jnp.float32)
        right = in_ref[meta_ref[here + 1]].astype(jnp.float32)
        out_ref[span] = (left + right).astype(jnp.bfloat16)
        return carry

    out_ref[0] = jnp.zeros(out_ref.shape[1:], jnp.bfloat16)
    lax.fori_loop(1, out_ref.shape[0], body, 0, unroll=9)


def paired(stripes_ref, which, pair, slot, heads):
    nothing = jnp.zeros((CH, HD), jnp.bfloat16)
    blocks = []
    for head in (2 * pair, 2 * pair + 1):
        at = (which * heads + head) * 2
        blocks.append(jnp.concatenate([stripes_ref[at, slot], stripes_ref[at + 1, slot]], axis=0))
    return jnp.concatenate(
        [
            jnp.concatenate([blocks[0], nothing], axis=1),
            jnp.concatenate([nothing, blocks[1]], axis=1),
        ],
        axis=0,
    )


def dot(left, right, left_dim, right_dim):
    return lax.dot_general(
        left, right, (((left_dim,), (right_dim,)), ((), ())), preferred_element_type=jnp.float32
    )


def stats_of(stripes_ref, enc_ref, out_ref):
    heads = enc_ref.shape[3] // HD
    pairs = heads // 2
    for slot in range(enc_ref.shape[1]):
        for pair in range(pairs):
            cols = slice(pair * 2 * HD, (pair + 1) * 2 * HD)
            queries = paired(stripes_ref, 0, pair, slot, heads)
            grads = paired(stripes_ref, 1, pair, slot, heads)
            scores = dot(enc_ref[0, slot, :, cols], queries, 1, 1) * SCALE
            d_weights = dot(enc_ref[1, slot, :, cols], grads, 1, 1)
            top = jnp.max(scores, axis=0, keepdims=True)
            powers = jnp.exp(scores - top)
            total = jnp.sum(powers, axis=0, keepdims=True)
            out_ref[0, slot, pair : pair + 1] = top + jnp.log(total)
            delta = jnp.sum(powers * d_weights, axis=0, keepdims=True) / total
            out_ref[0, slot, pairs + pair : pairs + pair + 1] = delta
    for dest in range(1, out_ref.shape[0]):
        out_ref[dest] = out_ref[0]


def joined(mine, other, sink):
    pairs = sink.shape[0]
    log_a, log_b = mine[:pairs], other[:pairs]
    top = jnp.maximum(jnp.maximum(log_a, log_b), sink)
    part_a, part_b, part_s = jnp.exp(log_a - top), jnp.exp(log_b - top), jnp.exp(sink - top)
    total = part_a + part_b + part_s
    deltas = (part_a * mine[pairs:] + part_b * other[pairs:]) / total
    return top + jnp.log(total), deltas, part_s / total


def slot_stats(meta_ref, stats_ref, sink_ref, slot, me_at):
    mine_at = meta_ref[me_at] + slot
    code = meta_ref[mine_at]
    live = ((code >> 6) & 1).astype(jnp.float32)
    log_total, deltas, _ = joined(stats_ref[mine_at], stats_ref[code >> 7], sink_ref[...])
    return log_total, deltas, live


def token_side(
    meta_ref, stripes_ref, enc_ref, stats_ref, sink_ref, out_ref, weights_ref, scores_ref, *, me_at
):
    heads = enc_ref.shape[3] // HD
    pairs = heads // 2
    slots = enc_ref.shape[1]
    for slot in range(slots):
        log_total, deltas, live = slot_stats(meta_ref, stats_ref, sink_ref, slot, me_at)
        spare = jnp.zeros((8 - 2 * pairs, 2 * CH), jnp.float32)
        columns = jnp.concatenate([log_total, deltas, spare], axis=0).T
        for pair in range(pairs):
            cols = slice(pair * 2 * HD, (pair + 1) * 2 * HD)
            queries = paired(stripes_ref, 0, pair, slot, heads)
            grads = paired(stripes_ref, 1, pair, slot, heads)
            scores = dot(queries, enc_ref[0, slot, :, cols], 1, 1) * SCALE
            d_weights = dot(grads, enc_ref[1, slot, :, cols], 1, 1)
            weights = jnp.exp(scores - columns[:, pair : pair + 1]) * live
            d_scores = weights * (d_weights - columns[:, pairs + pair : pairs + pair + 1]) * SCALE
            weights_ref[slot * pairs + pair] = weights.astype(jnp.bfloat16)
            scores_ref[slot * pairs + pair] = d_scores.astype(jnp.bfloat16)
    for slot in range(slots):
        for pair in range(pairs):
            cols = slice(pair * 2 * HD, (pair + 1) * 2 * HD)
            for which, ref in enumerate((weights_ref, scores_ref)):
                right = enc_ref[1 - which, slot, :, cols]
                rows = dot(ref[slot * pairs + pair], right, 1, 0).astype(jnp.bfloat16)
                for side in range(2):
                    for half in range(2):
                        stripe = (which * heads + 2 * pair + side) * 2 + half
                        at = side * CH + half * HALF
                        out_ref[stripe, slot] = rows[at : at + HALF, side * HD : (side + 1) * HD]


def slot_side(
    meta_ref, stripes_ref, enc_ref, stats_ref, sink_ref, out_ref, weights_ref, scores_ref, *, me_at
):
    heads = enc_ref.shape[3] // HD
    pairs = heads // 2
    count = out_ref.shape[1]
    first = pl.program_id(0) * count
    for step in range(count):
        slot = first + step
        log_total, deltas, live = slot_stats(meta_ref, stats_ref, sink_ref, slot, me_at)
        for pair in range(pairs):
            cols = slice(pair * 2 * HD, (pair + 1) * 2 * HD)
            queries = paired(stripes_ref, 0, pair, slot, heads)
            grads = paired(stripes_ref, 1, pair, slot, heads)
            scores = dot(enc_ref[0, slot, :, cols], queries, 1, 1) * SCALE
            d_weights = dot(enc_ref[1, slot, :, cols], grads, 1, 1)
            weights = jnp.exp(scores - log_total[pair : pair + 1]) * live
            d_scores = weights * (d_weights - deltas[pair : pair + 1]) * SCALE
            weights_ref[step * pairs + pair] = weights.astype(jnp.bfloat16)
            scores_ref[step * pairs + pair] = d_scores.astype(jnp.bfloat16)
    for step in range(count):
        slot = first + step
        for pair in range(pairs):
            cols = slice(pair * 2 * HD, (pair + 1) * 2 * HD)
            for which, ref in enumerate((scores_ref, weights_ref)):
                right = paired(stripes_ref, which, pair, slot, heads)
                rows = dot(ref[step * pairs + pair], right, 1, 0)
                out_ref[which, step, :, cols] = rows.astype(jnp.bfloat16)


def sink_side(meta_ref, stats_ref, sink_ref, out_ref, *, pos_at, live_at, spans):
    sink = sink_ref[...]

    def body(span, total):
        here = pos_at + 2 * span - NB
        live = meta_ref[live_at + span].astype(jnp.float32)
        _, deltas, part = joined(stats_ref[meta_ref[here]], stats_ref[meta_ref[here + 1]], sink)
        return total - part * deltas * live

    out_ref[...] = lax.fori_loop(1, spans, body, jnp.zeros_like(sink), unroll=7)


def routing(owner_row, doc_row, seq_index, slots, seq_count):
    neigh_count, spans = owner_row.shape[0], doc_row.shape[0]
    neigh_ids = jnp.arange(neigh_count, dtype=jnp.int32)
    before = neigh_ids[None, :] < neigh_ids[:, None]
    same_owner = owner_row[None, :] == owner_row[:, None]
    slot_of = jnp.sum(before & same_owner, axis=1).astype(jnp.int32)
    place = owner_row * slots + slot_of
    other = jnp.flip(place.reshape(spans, NB), axis=1).reshape(-1)
    span_ids = jnp.arange(spans, dtype=jnp.int32)
    live = ((span_ids >= 1) & (doc_row == 0)).astype(jnp.int32)
    next_live = jnp.concatenate([live[1:], jnp.zeros((1,), jnp.int32)])
    reader = jnp.minimum(neigh_ids // NB + 1, spans - 1)
    code = reader + 64 * jnp.repeat(next_live, NB) + 128 * other
    flat = jnp.arange(slots * seq_count, dtype=jnp.int32)
    codes = jnp.sum(jnp.where(place[None, :] == flat[:, None], code[None, :], 0), axis=1)
    first = (seq_index * slots).astype(jnp.int32).reshape(1)
    return jnp.concatenate([codes, place, live, first])


def on_device(queries, encodings, sink, owner, doc_start, d_out):
    seq_count = lax.axis_size("seq")
    seq_index = lax.axis_index("seq")
    tokens, width = queries.shape[1:]
    spans_here = tokens // CH
    heads = width // HD
    pairs = heads // 2
    slots = encodings.shape[2]
    spans, neighs = doc_start.shape[1], owner.shape[1]
    places = seq_count * slots
    pos_at = places
    live_at = pos_at + neighs
    me_at = live_at + spans
    bf16 = jnp.bfloat16
    f32 = jnp.float32
    stripe = (HALF, HD)
    tile = pltpu.VMEM((slots * pairs, NL, NL), bf16)
    flops = 4 * NL * CH * width * slots

    def everywhere(block):
        return lax.all_to_all(block, "seq", split_axis=0, concat_axis=0, tiled=True)

    def call(kernel, name, out, *operands, grid=(), out_specs=IN_VMEM, limit=16, work=0, **kw):
        return pl.pallas_call(
            kernel,
            grid=grid,
            in_specs=[IN_SMEM if x.dtype == jnp.int32 else IN_VMEM for x in operands],
            out_specs=out_specs,
            out_shape=out,
            compiler_params=pltpu.CompilerParams(vmem_limit_bytes=limit * MIB),
            cost_estimate=pl.CostEstimate(
                flops=work, bytes_accessed=sum(x.nbytes for x in operands), transcendentals=0
            ),
            name=name,
            **kw,
        )(*operands)

    meta = routing(owner[0], doc_start[0], seq_index, slots, seq_count)
    sink_rows = jnp.repeat(sink.reshape(pairs, 2), CH, axis=1)
    enc = encodings[0]

    def struct(shape, dtype=bf16):
        return jax.ShapeDtypeStruct(shape, dtype)

    cut = call(cut_stripes, "cut", struct((seq_count, spans_here) + stripe), queries[0], d_out[0])
    all_spans = everywhere(cut).reshape((spans,) + stripe)
    spread = call(spread_spans, "spread", struct((places,) + stripe), meta, all_spans)
    stripes = everywhere(spread.reshape((seq_count, slots) + stripe))
    stats = call(
        stats_of, "stats", struct((seq_count, slots, heads, HD), f32), stripes, enc, work=flops
    )
    all_stats = everywhere(stats).reshape(places, heads, HD)
    whole = (meta, stripes, enc, all_stats, sink_rows)
    partials = call(
        functools.partial(token_side, me_at=me_at),
        "token_side",
        struct(stripes.shape),
        *whole,
        work=2 * flops,
        scratch_shapes=[tile, tile],
    )
    returned = everywhere(partials).reshape((places,) + stripe)
    step = slots // GRAD_STEPS
    enc_grads = call(
        functools.partial(slot_side, me_at=me_at),
        "slot_side",
        struct(enc.shape),
        *whole,
        grid=(GRAD_STEPS,),
        out_specs=pl.BlockSpec((2, step, NL, width), lambda i: (0, i, 0, 0)),
        work=2 * flops,
        scratch_shapes=[pltpu.VMEM((step * pairs, NL, NL), bf16)] * 2,
    )
    sink_lanes = call(
        functools.partial(sink_side, pos_at=pos_at, live_at=live_at, spans=spans),
        "sink_side",
        struct((pairs, HD), f32),
        meta,
        all_stats,
        sink_rows,
        work=spans * 4096,
    )
    sink_part = jnp.sum(sink_lanes.reshape(heads, CH), axis=1)
    sink_total = sink_part + lax.ppermute(sink_part, "dp", [(0, 1), (1, 0)])
    returned, enc_grads, sink_total = lax.optimization_barrier((returned, enc_grads, sink_total))

    summed = call(
        functools.partial(add_partials, pos_at=pos_at),
        "add_partials",
        struct((spans,) + stripe),
        meta,
        returned,
    )
    final = everywhere(summed.reshape((seq_count, spans_here) + stripe))
    rows = pl.BlockSpec((tokens, width), lambda: (0, 0))
    attended, grad_query = call(
        join_stripes, "join", [struct((tokens, width))] * 2, final, out_specs=[rows, rows]
    )
    return attended[None], grad_query[None], enc_grads[None], sink_total


def solution(mesh):
    in_specs = (
        P("dp", "seq", "mp"),
        P("dp", None, "seq", None, "mp"),
        P("mp"),
        P("dp", None),
        P("dp", None),
        P("dp", "seq", "mp"),
    )
    out_specs = (
        P("dp", "seq", "mp"),
        P("dp", "seq", "mp"),
        P("dp", None, "seq", None, "mp"),
        P("mp"),
    )
    return jax.shard_map(
        on_device, mesh=mesh, in_specs=in_specs, out_specs=out_specs, check_vma=False
    )
```

time: 145 us -> 125 us (0.86)
  Pallas kernels: 40.5 us -> 15.4 us
  waiting for transfers between devices: 16.8 us -> 30.5 us
  blocking collectives: 60.3 us -> 47.7 us
  local copies, waits for them, and re-layouts: 4.72 us -> 8.7 us
    pallas_call x8, Pallas kernels: 40.5 us -> 15.4 us  [call(): pl.pallas_call(kernel, grid=grid, in_specs=[IN_SMEM if x.dtype == jnp.int...]
    all_to_all x3, waiting for transfers between devices: 16.8 us -> 30.5 us  [everywhere(): return lax.all_to_all(block, 'seq', split_axis=0, concat_axis=0, tiled=True)]
    all_to_all x2, blocking collectives: 60.3 us -> 47.7 us  [everywhere(): return lax.all_to_all(block, 'seq', split_axis=0, concat_axis=0, tiled=True)]
    unnamed x12 -> x18, local copies, waits for them, and re-layouts: 2.39 us -> 7.6 us
  transfers between devices with their start and end apart: 4 -> 4, of which waited for: 2 -> 3; matrix products, arithmetic and copies ran while one was open for 3% -> 2% of each run, Pallas kernels for 9% -> 5%
where the time goes in v2:
time: 125 us; the launch traced here: 124 us
  blocking collectives  47.7 us (38%)
  waiting for transfers between devices  30.5 us (24%)
  starting transfers between devices  19.3 us (15%)
  Pallas kernels  15.4 us (12%)
  local copies, waits for them, and re-layouts  8.7 us (7%)
    all_to_all x2, blocking collectives, everywhere(): return lax.all_to_all(block, 'seq', split_axis=0, concat_axis=0, tiled=True)  47.7 us
    all_to_all x3, waiting for transfers between devices, everywhere(): return lax.all_to_all(block, 'seq', split_axis=0, concat_axis=0, tiled=True)  30.5 us
    all_to_all x3, starting transfers between devices, everywhere(): return lax.all_to_all(block, 'seq', split_axis=0, concat_axis=0, tiled=True)  15.6 us
    pallas_call x8, Pallas kernels, call(): pl.pallas_call(kernel, grid=grid, in_specs=[IN_SMEM if x.dtype == jnp.int...  15.4 us
    unnamed x18, local copies, waits for them, and re-layouts  7.6 us
    ppermute x1, starting transfers between devices, on_device(): sink_total = sink_part + lax.ppermute(sink_part, 'dp', [(0, 1), (1, 0)])  3.75 us
  transfers between devices with their start and end apart: 4, of which 3 were waited for; matrix products, arithmetic and copies ran while one was open for 2% of the time, Pallas kernels for 5%

profile of v2, /device:TPU:1, one launch (start us, length us, event | category | flops | bytes accessed | tf_op | source)
XLA Modules:
  0.0 123.6 jit_solution(1239479813393630642)
XLA Ops:
  0.7 1.0 copy-done.4
  1.6 0.9 copy-done.5
  2.6 0.9 cut.1
  3.4 7.6 %all-to-all-start = ((bf16[16,4,32,128]{3,2,1,0:T(8,128)(2,1)}), bf16[16,4,32,128]{3,2,1,0:T(8,128)(2,1)S(1)}, u32[]{:S(2)}, u32[]{:S(2)}) async-start(bf16[16,4,32,128]{3,2,1,0:T(8,128)(2,1)} %cut.1), calls=%async_computation | async-start | bytes 1048576 | tf_op jit(solution)/shard_map/all_to_all | solution.py:237
  11.1 0.2 convert_reduce_fusion
  11.2 0.1 reduce_sum.33
  11.4 0.1 mul.50
  11.6 0.1 mul.53
  12.0 0.1 mul.49
  12.2 0.1 select_reduce_fusion
  12.4 9.2 %all-to-all-done = bf16[16,4,32,128]{3,2,1,0:T(8,128)(2,1)S(1)} async-done(((bf16[16,4,32,128]{3,2,1,0:T(8,128)(2,1)}), bf16[16,4,32,128]{3,2,1,0:T(8,128)(2,1)S(1)}, u32[]{:S(2)}, u32[]{:S(2)}) %all-to-all-start) | async-done | bytes 524320 | tf_op jit(solution)/shard_map/all_to_all | solution.py:237
  21.6 1.0 spread.1
  22.5 30.2 %all_to_all.25.stripes_ref = bf16[16,16,32,128]{3,2,1,0:T(8,128)(2,1)S(1)} all-to-all(bf16[16,16,32,128]{3,2,1,0:T(8,128)(2,1)S(1)} %bitcast.27), channel_id=1, replica_groups=mesh['seq'=16,'mp'=8,'dp'=2] {'seq'}, dimensions={0} | all-to-all | bytes 4194304 | tf_op jit(solution)/shard_map/all_to_all | solution.py:237
  52.8 2.2 %stats.1 = f32[16,16,4,128]{3,2,1,0:T(4,128)} custom-call(bf16[16,16,32,128]{3,2,1,0:T(8,128)(2,1)S(1)} %all_to_all.25.stripes_ref, bf16[2,16,128,512]{3,2,1,0:T(8,128)(2,1)S(1)} %bitcast.24), custom_call_target="tpu_custom_call" | custom-call | flops 268435456 | bytes 6291456 | tf_op jit(solution)/shard_map/stats/pallas_call | solution.py:240
  54.9 3.6 %all-to-all-start.2 = ((f32[16,16,4,128]{3,2,1,0:T(4,128)}), f32[16,16,4,128]{3,2,1,0:T(4,128)S(1)}, u32[]{:S(2)}, u32[]{:S(2)}) async-start(f32[16,16,4,128]{3,2,1,0:T(4,128)} %stats.1), calls=%async_computation.2 | async-start | bytes 1048576 | tf_op jit(solution)/shard_map/all_to_all | solution.py:237
  58.5 0.1 reshape.81
  58.7 0.1 reshape.82.sink_ref
  58.8 8.9 %all-to-all-done.2 = f32[16,16,4,128]{3,2,1,0:T(4,128)S(1)} async-done(((f32[16,16,4,128]{3,2,1,0:T(4,128)}), f32[16,16,4,128]{3,2,1,0:T(4,128)S(1)}, u32[]{:S(2)}, u32[]{:S(2)}) %all-to-all-start.2) | async-done | bytes 524320 | tf_op jit(solution)/shard_map/all_to_all | solution.py:237
  67.6 2.2 %copy-done.1 = bf16[1,2,16,128,512]{4,3,2,1,0:T(8,128)(2,1)S(1)} copy-done((bf16[1,2,16,128,512]{4,3,2,1,0:T(8,128)(2,1)S(1)}, bf16[1,2,16,128,512]{4,3,2,1,0:T(8,128)(2,1)}, u32[]{:S(2)}) %copy-start.1) | copy-done | bytes 4194328
  69.8 3.0 %token_side.1 = bf16[16,16,32,128]{3,2,1,0:T(8,128)(2,1)S(1)} custom-call(s32[449]{0:T(512)S(1)} %pad_add_fusion.meta_ref, bf16[16,16,32,128]{3,2,1,0:T(8,128)(2,1)S(1)} %all_to_all.25.stripes_ref, bf16[2,16,128,512]{3,2,1,0:T(8,128)(2,1)S(1)} %bitcast.25, f32[256,4,128]{2,1,0:T(4,128)S(1)} %bitcast.28, f32[2,128]{1,0:T(2,128)S(1)} %reshape.82.sink_ref), custom_call_target="tpu_custom_call" | custom-call | flops 536870912 | bytes 6818564 | tf_op jit(solution)/shard_map/token_side/pallas_call | solution.py:240
  72.9 1.3 %copy-done.3 = bf16[16,16,32,128]{3,2,1,0:T(8,128)(2,1)} copy-done((bf16[16,16,32,128]{3,2,1,0:T(8,128)(2,1)}, bf16[16,16,32,128]{3,2,1,0:T(8,128)(2,1)S(1)}, u32[]{:S(2)}) %copy-start.3) | copy-done | bytes 2097176
  74.2 4.4 %all-to-all-start.3 = ((bf16[16,16,32,128]{3,2,1,0:T(8,128)(2,1)}), bf16[16,16,32,128]{3,2,1,0:T(8,128)(2,1)}, u32[]{:S(2)}, u32[]{:S(2)}) async-start(bf16[16,16,32,128]{3,2,1,0:T(8,128)(2,1)} %copy-done.3), calls=%async_computation.3 | async-start | bytes 4194304 | tf_op jit(solution)/shard_map/all_to_all | solution.py:237
  78.6 1.0 sink_side.1
  79.7 0.1 reduce_sum.35
  79.8 3.7 %collective-permute-start = (f32[4]{0:T(128)S(1)}, f32[4]{0:T(128)S(1)}, u32[]{:S(2)}, u32[]{:S(2)}) collective-permute-start(f32[4]{0:T(128)S(1)} %reduce_sum.35), channel_id=1, source_target_pairs={{0,1},{1,0},{2,3},{3,2},{4,5},{5,4},{6,7},{7,6},{8,9},{9,8},{10,11... | collective-permute-start | bytes 56 | tf_op jit(solution)/shard_map/ppermute | solution.py:300
  83.5 2.2 %copy-done.2 = bf16[1,2,16,128,512]{4,3,2,1,0:T(8,128)(2,1)S(1)} copy-done((bf16[1,2,16,128,512]{4,3,2,1,0:T(8,128)(2,1)S(1)}, bf16[1,2,16,128,512]{4,3,2,1,0:T(8,128)(2,1)}, u32[]{:S(2)}) %copy-start.2) | copy-done | bytes 4194328
  85.7 4.7 %slot_side.1 = bf16[2,16,128,512]{3,2,1,0:T(8,128)(2,1)} custom-call(s32[449]{0:T(512)S(1)} %pad_add_fusion.meta_ref, bf16[16,16,32,128]{3,2,1,0:T(8,128)(2,1)S(1)} %all_to_all.25.stripes_ref, bf16[2,16,128,512]{3,2,1,0:T(8,128)(2,1)S(1)} %bitcast.26, f32[256,4,128]{2,1,0:T(4,128)S(1)} %bitcast.30, f32[2,128]{1,0:T(2,128)S(1)} %reshape.82.sink_ref), custom_call_target="tpu_custom_call" | custom-call | flops 536870912 | bytes 6818564 | tf_op jit(solution)/shard_map/slot_side/pallas_call | solution.py:240
  90.4 0.5 add.45
  90.9 12.5 %all-to-all-done.3 = bf16[16,16,32,128]{3,2,1,0:T(8,128)(2,1)} async-done(((bf16[16,16,32,128]{3,2,1,0:T(8,128)(2,1)}), bf16[16,16,32,128]{3,2,1,0:T(8,128)(2,1)}, u32[]{:S(2)}, u32[]{:S(2)}) %all-to-all-start.3) | async-done | bytes 2097184 | tf_op jit(solution)/shard_map/all_to_all | solution.py:237
  103.4 1.8 %add_partials.1 = bf16[64,32,128]{2,1,0:T(8,128)(2,1)S(1)} custom-call(s32[449]{0:T(512)S(1)} %pad_add_fusion.meta_ref, bf16[256,32,128]{2,1,0:T(8,128)(2,1)} %bitcast.11.in_ref), custom_call_target="tpu_custom_call" | custom-call | bytes 2098948 | tf_op jit(solution)/shard_map/add_partials/pallas_call | solution.py:240
  105.2 17.5 %all_to_all.26.in_ref = bf16[16,4,32,128]{3,2,1,0:T(8,128)(2,1)S(1)} all-to-all(bf16[16,4,32,128]{3,2,1,0:T(8,128)(2,1)S(1)} %bitcast.32), channel_id=1, replica_groups=mesh['seq'=16,'mp'=8,'dp'=2] {'seq'}, dimensions={0} | all-to-all | bytes 1048576 | tf_op jit(solution)/shard_map/all_to_all | solution.py:237
  122.7 0.9 join.1
  (27 shorter events, 0.6 us)
Async XLA Ops:
  0.6 10.4 %copy-start.6 = (s32[1,128]{1,0:T(1,128)S(1)}, s32[1,128]{1,0:T(1,128)}, u32[]{:S(2)}) copy-start(s32[1,128]{1,0:T(1,128)} %param.9) | copy-start | bytes 1540
  0.6 10.8 %copy-start.7 = (s32[1,64]{1,0:T(1,128)S(1)}, s32[1,64]{1,0:T(1,128)}, u32[]{:S(2)}) copy-start(s32[1,64]{1,0:T(1,128)} %param.10) | copy-start | bytes 772
  0.7 1.0 copy-start.4
  1.6 0.9 copy-start.5
  3.4 18.1 %all-to-all-start = ((bf16[16,4,32,128]{3,2,1,0:T(8,128)(2,1)}), bf16[16,4,32,128]{3,2,1,0:T(8,128)(2,1)S(1)}, u32[]{:S(2)}, u32[]{:S(2)}) async-start(bf16[16,4,32,128]{3,2,1,0:T(8,128)(2,1)} %cut.1), calls=%async_computation | async-start | bytes 1048576 | tf_op jit(solution)/shard_map/all_to_all | solution.py:237
  22.5 30.2 %copy-start = (bf16[1,2,16,128,512]{4,3,2,1,0:T(8,128)(2,1)S(1)}, bf16[1,2,16,128,512]{4,3,2,1,0:T(8,128)(2,1)}, u32[]{:S(2)}) copy-start(bf16[1,2,16,128,512]{4,3,2,1,0:T(8,128)(2,1)} %param.7) | copy-start | bytes 12582916
  52.8 5.7 %copy-start.8 = (f32[4]{0:T(128)S(1)}, f32[4]{0:T(128)}, u32[]{:S(2)}) copy-start(f32[4]{0:T(128)} %param.8) | copy-start | bytes 52
  54.9 12.7 %all-to-all-start.2 = ((f32[16,16,4,128]{3,2,1,0:T(4,128)}), f32[16,16,4,128]{3,2,1,0:T(4,128)S(1)}, u32[]{:S(2)}, u32[]{:S(2)}) async-start(f32[16,16,4,128]{3,2,1,0:T(4,128)} %stats.1), calls=%async_computation.2 | async-start | bytes 1048576 | tf_op jit(solution)/shard_map/all_to_all | solution.py:237
  67.6 2.2 %copy-start.1 = (bf16[1,2,16,128,512]{4,3,2,1,0:T(8,128)(2,1)S(1)}, bf16[1,2,16,128,512]{4,3,2,1,0:T(8,128)(2,1)}, u32[]{:S(2)}) copy-start(bf16[1,2,16,128,512]{4,3,2,1,0:T(8,128)(2,1)} %param.7) | copy-start | bytes 12582916
  72.9 1.3 %copy-start.3 = (bf16[16,16,32,128]{3,2,1,0:T(8,128)(2,1)}, bf16[16,16,32,128]{3,2,1,0:T(8,128)(2,1)S(1)}, u32[]{:S(2)}) copy-start(bf16[16,16,32,128]{3,2,1,0:T(8,128)(2,1)S(1)} %token_side.1) | copy-start | bytes 6291460
  74.2 29.2 %all-to-all-start.3 = ((bf16[16,16,32,128]{3,2,1,0:T(8,128)(2,1)}), bf16[16,16,32,128]{3,2,1,0:T(8,128)(2,1)}, u32[]{:S(2)}, u32[]{:S(2)}) async-start(bf16[16,16,32,128]{3,2,1,0:T(8,128)(2,1)} %copy-done.3), calls=%async_computation.3 | async-start | bytes 4194304 | tf_op jit(solution)/shard_map/all_to_all | solution.py:237
  79.8 10.6 %collective-permute-start = (f32[4]{0:T(128)S(1)}, f32[4]{0:T(128)S(1)}, u32[]{:S(2)}, u32[]{:S(2)}) collective-permute-start(f32[4]{0:T(128)S(1)} %reduce_sum.35), channel_id=1, source_target_pairs={{0,1},{1,0},{2,3},{3,2},{4,5},{5,4},{6,7},{7,6},{8,9},{9,8},{10,11... | collective-permute-start | bytes 56 | tf_op jit(solution)/shard_map/ppermute | solution.py:300
  83.5 2.2 %copy-start.2 = (bf16[1,2,16,128,512]{4,3,2,1,0:T(8,128)(2,1)S(1)}, bf16[1,2,16,128,512]{4,3,2,1,0:T(8,128)(2,1)}, u32[]{:S(2)}) copy-start(bf16[1,2,16,128,512]{4,3,2,1,0:T(8,128)(2,1)} %param.7) | copy-start | bytes 12582916

commit v3 on v2

--- a/solution.py
+++ b/solution.py
@@ -14,20 +14,33 @@
 HALF = CH // 2
 SCALE = HD ** (-0.5)
 MIB = 1024 * 1024
-GRAD_STEPS = 4
+STEPS = 2
 IN_VMEM = pl.BlockSpec(memory_space=pltpu.VMEM)
+IN_HBM = pl.BlockSpec(memory_space=pltpu.HBM)
 IN_SMEM = pl.BlockSpec(memory_space=pltpu.SMEM)
 
 
-def cut_stripes(query_ref, grad_ref, out_ref):
-    spans, heads = out_ref.shape[1], query_ref.shape[1] // HD
-    for which, ref in enumerate((query_ref, grad_ref)):
+def cut_stripes(query_hbm, grad_hbm, out_hbm, rows_ref, out_ref, in_sems, out_sems):
+    whiches, heads, halves, spans = out_ref.shape[:4]
+    loads, stores = [], []
+    for which, ref in enumerate((query_hbm, grad_hbm)):
+        loads.append(pltpu.make_async_copy(ref, rows_ref.at[which], in_sems.at[which]))
+        stores.append(
+            pltpu.make_async_copy(out_ref.at[which], out_hbm.at[which], out_sems.at[which])
+        )
+        loads[which].start()
+    for which in range(whiches):
+        loads[which].wait()
         for head in range(heads):
-            for half in range(2):
-                stripe = (which * heads + head) * 2 + half
+            for half in range(halves):
                 for span in range(spans):
                     row = span * CH + half * HALF
-                    out_ref[stripe, span] = ref[row : row + HALF, head * HD : (head + 1) * HD]
+                    out_ref[which, head, half, span] = rows_ref[
+                        which, row : row + HALF, head * HD : (head + 1) * HD
+                    ]
+        stores[which].start()
+    for store in stores:
+        store.wait()
 
 
 def join_stripes(in_ref, attended_ref, query_ref):
@@ -41,7 +54,7 @@
                     ref[row : row + HALF, head * HD : (head + 1) * HD] = in_ref[stripe, span]
 
 
-def spread_spans(meta_ref, in_ref, out_ref):
+def spread_spans(meta_ref, in_ref, sink_ref, out_ref):
     def body(i, carry):
         out_ref[i] = in_ref[meta_ref[i] & 63]
         return carry
@@ -50,6 +63,7 @@
 
 
 def add_partials(meta_ref, in_ref, out_ref, *, pos_at):
+
     def body(span, carry):
         here = pos_at + 2 * span - NB
         left = in_ref[meta_ref[here]].astype(jnp.float32)
@@ -85,7 +99,10 @@
 def stats_of(stripes_ref, enc_ref, out_ref):
     heads = enc_ref.shape[3] // HD
     pairs = heads // 2
-    for slot in range(enc_ref.shape[1]):
+    count = out_ref.shape[1]
+    first = pl.program_id(0) * count
+    for step in range(count):
+        slot = first + step
         for pair in range(pairs):
             cols = slice(pair * 2 * HD, (pair + 1) * 2 * HD)
             queries = paired(stripes_ref, 0, pair, slot, heads)
@@ -95,9 +112,9 @@
             top = jnp.max(scores, axis=0, keepdims=True)
             powers = jnp.exp(scores - top)
             total = jnp.sum(powers, axis=0, keepdims=True)
-            out_ref[0, slot, pair : pair + 1] = top + jnp.log(total)
+            out_ref[0, step, pair : pair + 1] = top + jnp.log(total)
             delta = jnp.sum(powers * d_weights, axis=0, keepdims=True) / total
-            out_ref[0, slot, pairs + pair : pairs + pair + 1] = delta
+            out_ref[0, step, pairs + pair : pairs + pair + 1] = delta
     for dest in range(1, out_ref.shape[0]):
         out_ref[dest] = out_ref[0]
 
@@ -154,8 +171,9 @@
 
 
 def slot_side(
-    meta_ref, stripes_ref, enc_ref, stats_ref, sink_ref, out_ref, weights_ref, scores_ref, *, me_at
+    meta_ref, stripes_ref, enc_ref, stats_ref, sink_ref, after_ref, *refs, me_at
 ):
+    out_ref, weights_ref, scores_ref = refs
     heads = enc_ref.shape[3] // HD
     pairs = heads // 2
     count = out_ref.shape[1]
@@ -183,7 +201,7 @@
                 out_ref[which, step, :, cols] = rows.astype(jnp.bfloat16)
 
 
-def sink_side(meta_ref, stats_ref, sink_ref, out_ref, *, pos_at, live_at, spans):
+def sink_side(meta_ref, stats_ref, sink_ref, after_ref, out_ref, *, pos_at, live_at, spans):
     sink = sink_ref[...]
 
     def body(span, total):
@@ -230,17 +248,17 @@
     bf16 = jnp.bfloat16
     f32 = jnp.float32
     stripe = (HALF, HD)
-    tile = pltpu.VMEM((slots * pairs, NL, NL), bf16)
     flops = 4 * NL * CH * width * slots
 
     def everywhere(block):
         return lax.all_to_all(block, "seq", split_axis=0, concat_axis=0, tiled=True)
 
-    def call(kernel, name, out, *operands, grid=(), out_specs=IN_VMEM, limit=16, work=0, **kw):
+    def call(kernel, name, out, *operands, in_specs=None, out_specs=IN_VMEM, work=0, limit=16, **kw):
+        if in_specs is None:
+            in_specs = [IN_SMEM if x.dtype == jnp.int32 else IN_VMEM for x in operands]
         return pl.pallas_call(
             kernel,
-            grid=grid,
-            in_specs=[IN_SMEM if x.dtype == jnp.int32 else IN_VMEM for x in operands],
+            in_specs=in_specs,
             out_specs=out_specs,
             out_shape=out,
             compiler_params=pltpu.CompilerParams(vmem_limit_bytes=limit * MIB),
@@ -249,7 +267,7 @@
             ),
             name=name,
             **kw,
-        )(*operands)
+        )(*(in_hbm(x) if spec is IN_HBM else x for x, spec in zip(operands, in_specs)))
 
     meta = routing(owner[0], doc_start[0], seq_index, slots, seq_count)
     sink_rows = jnp.repeat(sink.reshape(pairs, 2), CH, axis=1)
@@ -258,12 +276,50 @@
     def struct(shape, dtype=bf16):
         return jax.ShapeDtypeStruct(shape, dtype)
 
-    cut = call(cut_stripes, "cut", struct((seq_count, spans_here) + stripe), queries[0], d_out[0])
-    all_spans = everywhere(cut).reshape((spans,) + stripe)
-    spread = call(spread_spans, "spread", struct((places,) + stripe), meta, all_spans)
+    def in_hbm(x):
+        return pltpu.with_memory_space_constraint(x, pltpu.HBM)
+
+    def by_slots(shape, axis):
+        block = tuple(n // STEPS if d == axis else n for d, n in enumerate(shape))
+        return pl.BlockSpec(block, lambda i: tuple(i if d == axis else 0 for d in range(len(shape))))
+
+    cut_shape = (2, heads, 2, spans_here) + stripe
+    cut = call(
+        cut_stripes,
+        "cut",
+        pltpu.HBM(cut_shape, bf16),
+        queries[0],
+        d_out[0],
+        in_specs=[IN_HBM, IN_HBM],
+        out_specs=IN_HBM,
+        scratch_shapes=[
+            pltpu.VMEM((2, tokens, width), bf16),
+            pltpu.VMEM(cut_shape, bf16),
+            pltpu.SemaphoreType.DMA((2,)),
+            pltpu.SemaphoreType.DMA((2,)),
+        ],
+    )
+    all_spans = everywhere(cut.reshape((seq_count, spans_here) + stripe))
+    spread = call(
+        spread_spans,
+        "spread",
+        struct((places,) + stripe),
+        meta,
+        all_spans.reshape((spans,) + stripe),
+        sink_rows,
+    )
     stripes = everywhere(spread.reshape((seq_count, slots) + stripe))
+
+    stats_shape = (seq_count, slots, heads, HD)
     stats = call(
-        stats_of, "stats", struct((seq_count, slots, heads, HD), f32), stripes, enc, work=flops
+        stats_of,
+        "stats",
+        struct(stats_shape, f32),
+        stripes,
+        enc,
+        grid=(STEPS,),
+        out_specs=by_slots(stats_shape, 1),
+        work=flops,
     )
     all_stats = everywhere(stats).reshape(places, heads, HD)
     whole = (meta, stripes, enc, all_stats, sink_rows)
@@ -273,19 +329,28 @@
         struct(stripes.shape),
         *whole,
         work=2 * flops,
-        scratch_shapes=[tile, tile],
+        scratch_shapes=[pltpu.VMEM((slots * pairs, NL, NL), bf16)] * 2,
     )
     returned = everywhere(partials).reshape((places,) + stripe)
-    step = slots // GRAD_STEPS
+    summed = call(
+        functools.partial(add_partials, pos_at=pos_at),
+        "add_partials",
+        pltpu.HBM((spans,) + stripe, bf16),
+        meta,
+        returned,
+    )
+    final = everywhere(summed.reshape((seq_count, spans_here) + stripe))
     enc_grads = call(
         functools.partial(slot_side, me_at=me_at),
         "slot_side",
         struct(enc.shape),
         *whole,
-        grid=(GRAD_STEPS,),
-        out_specs=pl.BlockSpec((2, step, NL, width), lambda i: (0, i, 0, 0)),
+        summed,
+        in_specs=[IN_SMEM] + [IN_VMEM] * 4 + [IN_HBM],
+        grid=(STEPS,),
+        out_specs=by_slots(enc.shape, 1),
         work=2 * flops,
-        scratch_shapes=[pltpu.VMEM((step * pairs, NL, NL), bf16)] * 2,
+        scratch_shapes=[pltpu.VMEM((slots // STEPS * pairs, NL, NL), bf16)] * 2,
     )
     sink_lanes = call(
         functools.partial(sink_side, pos_at=pos_at, live_at=live_at, spans=spans),
@@ -294,20 +359,13 @@
         meta,
         all_stats,
         sink_rows,
+        summed,
+        in_specs=[IN_SMEM, IN_VMEM, IN_VMEM, IN_HBM],
         work=spans * 4096,
     )
     sink_part = jnp.sum(sink_lanes.reshape(heads, CH), axis=1)
     sink_total = sink_part + lax.ppermute(sink_part, "dp", [(0, 1), (1, 0)])
-    returned, enc_grads, sink_total = lax.optimization_barrier((returned, enc_grads, sink_total))
-
-    summed = call(
-        functools.partial(add_partials, pos_at=pos_at),
-        "add_partials",
-        struct((spans,) + stripe),
-        meta,
-        returned,
-    )
-    final = everywhere(summed.reshape((seq_count, spans_here) + stripe))
+
     rows = pl.BlockSpec((tokens, width), lambda: (0, 0))
     attended, grad_query = call(
         join_stripes, "join", [struct((tokens, width))] * 2, final, out_specs=[rows, rows]

time: 125 us -> 115 us (0.920)
  waiting for transfers between devices: 30.5 us -> 8.92 us
  blocking collectives: 47.7 us -> 68.8 us
  local copies, waits for them, and re-layouts: 8.7 us -> 3.3 us
  starting transfers between devices: 19.3 us -> 16.4 us
    all_to_all x3 -> x2, waiting for transfers between devices: 30.5 us -> 8.91 us  [everywhere(): return lax.all_to_all(block, 'seq', split_axis=0, concat_axis=0, tiled=True)]
    all_to_all x2 -> x3, blocking collectives: 47.7 us -> 68.8 us  [everywhere(): return lax.all_to_all(block, 'seq', split_axis=0, concat_axis=0, tiled=True)]
    unnamed x18 -> x10, local copies, waits for them, and re-layouts: 7.6 us -> 2.21 us
    all_to_all x3 -> x2, starting transfers between devices: 15.6 us -> 11.2 us  [everywhere(): return lax.all_to_all(block, 'seq', split_axis=0, concat_axis=0, tiled=True)]
    ppermute x1, starting transfers between devices: 3.75 us -> 5.22 us  [on_device(): sink_total = sink_part + lax.ppermute(sink_part, 'dp', [(0, 1), (1, 0)])]
  transfers between devices with their start and end apart: 4 -> 3, of which waited for: 3 -> 1; matrix products, arithmetic and copies ran while one was open for 2% -> 2% of each run, Pallas kernels for 5% -> 5%
where the time goes in v3:
time: 115 us
  blocking collectives  68.8 us (60%)
  starting transfers between devices  16.4 us (14%)
  Pallas kernels  15.3 us (13%)
  waiting for transfers between devices  8.92 us (8%)
  local copies, waits for them, and re-layouts  3.3 us (3%)
    all_to_all x3, blocking collectives, everywhere(): return lax.all_to_all(block, 'seq', split_axis=0, concat_axis=0, tiled=True)  68.8 us
    pallas_call x8, Pallas kernels, call(): pl.pallas_call(kernel, in_specs=in_specs, out_specs=out_specs, out_shape=...  15.3 us
    all_to_all x2, starting transfers between devices, everywhere(): return lax.all_to_all(block, 'seq', split_axis=0, concat_axis=0, tiled=True)  11.2 us
    all_to_all x2, waiting for transfers between devices, everywhere(): return lax.all_to_all(block, 'seq', split_axis=0, concat_axis=0, tiled=True)  8.91 us
    ppermute x1, starting transfers between devices, on_device(): sink_total = sink_part + lax.ppermute(sink_part, 'dp', [(0, 1), (1, 0)])  5.22 us
  transfers between devices with their start and end apart: 3, of which 1 were waited for; matrix products, arithmetic and copies ran while one was open for 2% of the time, Pallas kernels for 5%

profile of v3, /device:TPU:1, one launch (start us, length us, event | category | flops | bytes accessed | tf_op | source)
XLA Modules:
  0.0 114.7 jit_solution(4481365550486243849)
XLA Ops:
  0.7 1.8 %cut.1 = bf16[2,4,2,4,32,128]{5,4,3,2,1,0:T(8,128)(2,1)} custom-call(bf16[256,512]{1,0:T(8,128)(2,1)} %bitcast.37, bf16[256,512]{1,0:T(8,128)(2,1)} %bitcast.38), custom_call_target="tpu_custom_call" | custom-call | bytes 524288 | tf_op jit(solution)/shard_map/cut/pallas_call | solution.py:259
  2.5 7.6 %all-to-all-start = ((bf16[16,4,32,128]{3,2,1,0:T(8,128)(2,1)}), bf16[16,4,32,128]{3,2,1,0:T(8,128)(2,1)S(1)}, u32[]{:S(2)}, u32[]{:S(2)}) async-start(bf16[16,4,32,128]{3,2,1,0:T(8,128)(2,1)} %bitcast.36), calls=%async_computation | async-start | bytes 1048576 | tf_op jit(solution)/shard_map/all_to_all | solution.py:254
  10.1 0.2 convert_reduce_fusion
  10.3 0.1 reduce_sum.33
  10.5 0.1 mul.50
  10.6 0.1 rev.4
  10.7 0.1 mul.53
  10.9 0.1 add_multiply_fusion
  11.0 0.1 broadcast_in_dim.32
  11.1 0.1 mul.49
  11.3 0.1 reshape.83
  11.3 0.1 broadcast_in_dim.35
  11.4 0.1 reshape.84.sink_ref
  11.5 0.1 select_reduce_fusion
  11.6 0.1 pad_add_fusion.meta_ref
  11.7 8.9 %all-to-all-done = bf16[16,4,32,128]{3,2,1,0:T(8,128)(2,1)S(1)} async-done(((bf16[16,4,32,128]{3,2,1,0:T(8,128)(2,1)}), bf16[16,4,32,128]{3,2,1,0:T(8,128)(2,1)S(1)}, u32[]{:S(2)}, u32[]{:S(2)}) %all-to-all-start) | async-done | bytes 524320 | tf_op jit(solution)/shard_map/all_to_all | solution.py:254
  20.6 1.0 spread.1
  21.6 30.2 %all_to_all.25.stripes_ref = bf16[16,16,32,128]{3,2,1,0:T(8,128)(2,1)S(1)} all-to-all(bf16[16,16,32,128]{3,2,1,0:T(8,128)(2,1)S(1)} %bitcast.28), channel_id=1, replica_groups=mesh['seq'=16,'mp'=8,'dp'=2] {'seq'}, dimensions={0} | all-to-all | bytes 4194304 | tf_op jit(solution)/shard_map/all_to_all | solution.py:254
  51.8 1.6 %stats.1 = f32[16,16,4,128]{3,2,1,0:T(4,128)S(1)} custom-call(bf16[16,16,32,128]{3,2,1,0:T(8,128)(2,1)S(1)} %all_to_all.25.stripes_ref, bf16[2,16,128,512]{3,2,1,0:T(8,128)(2,1)S(1)} %bitcast.25), custom_call_target="tpu_custom_call" | custom-call | flops 268435456 | bytes 6291456 | tf_op jit(solution)/shard_map/stats/pallas_call | solution.py:259
  53.5 11.6 %all_to_all.26 = f32[16,16,4,128]{3,2,1,0:T(4,128)S(1)} all-to-all(f32[16,16,4,128]{3,2,1,0:T(4,128)S(1)} %stats.1), channel_id=1, replica_groups=mesh['seq'=16,'mp'=8,'dp'=2] {'seq'}, dimensions={0} | all-to-all | bytes 1048576 | tf_op jit(solution)/shard_map/all_to_all | solution.py:254
  65.1 3.1 %token_side.1 = bf16[16,16,32,128]{3,2,1,0:T(8,128)(2,1)S(1)} custom-call(s32[449]{0:T(512)S(1)} %pad_add_fusion.meta_ref, bf16[16,16,32,128]{3,2,1,0:T(8,128)(2,1)S(1)} %all_to_all.25.stripes_ref, bf16[2,16,128,512]{3,2,1,0:T(8,128)(2,1)S(1)} %bitcast.26, f32[256,4,128]{2,1,0:T(4,128)S(1)} %bitcast.30, f32[2,128]{1,0:T(2,128)S(1)} %reshape.84.sink_ref), custom_call_target="tpu_custom_call" | custom-call | flops 536870912 | bytes 6818564 | tf_op jit(solution)/shard_map/token_side/pallas_call | solution.py:259
  68.2 27.0 %all_to_all.27 = bf16[16,16,32,128]{3,2,1,0:T(8,128)(2,1)S(1)} all-to-all(bf16[16,16,32,128]{3,2,1,0:T(8,128)(2,1)S(1)} %token_side.1), channel_id=1, replica_groups=mesh['seq'=16,'mp'=8,'dp'=2] {'seq'}, dimensions={0} | all-to-all | bytes 4194304 | tf_op jit(solution)/shard_map/all_to_all | solution.py:254
  95.1 1.5 %add_partials.1.after_ref = bf16[64,32,128]{2,1,0:T(8,128)(2,1)} custom-call(s32[449]{0:T(512)S(1)} %pad_add_fusion.meta_ref, bf16[256,32,128]{2,1,0:T(8,128)(2,1)S(1)} %bitcast.29), custom_call_target="tpu_custom_call" | custom-call | bytes 2098948 | tf_op jit(solution)/shard_map/add_partials/pallas_call | solution.py:259
  96.7 3.6 %all-to-all-start.4 = ((bf16[16,4,32,128]{3,2,1,0:T(8,128)(2,1)}), bf16[16,4,32,128]{3,2,1,0:T(8,128)(2,1)S(1)}, u32[]{:S(2)}, u32[]{:S(2)}) async-start(bf16[16,4,32,128]{3,2,1,0:T(8,128)(2,1)} %bitcast.34), calls=%async_computation.4 | async-start | bytes 1048576 | tf_op jit(solution)/shard_map/all_to_all | solution.py:254
  100.3 1.0 sink_side.1
  101.2 0.1 reshape.89
  101.3 0.1 reduce_sum.35
  101.5 5.2 %collective-permute-start = (f32[4]{0:T(128)S(1)}, f32[4]{0:T(128)S(1)}, u32[]{:S(2)}, u32[]{:S(2)}) collective-permute-start(f32[4]{0:T(128)S(1)} %reduce_sum.35), channel_id=1, source_target_pairs={{0,1},{1,0},{2,3},{3,2},{4,5},{5,4},{6,7},{7,6},{8,9},{9,8},{10,11... | collective-permute-start | bytes 56 | tf_op jit(solution)/shard_map/ppermute | solution.py:367
  106.7 2.2 %copy-done.1 = bf16[1,2,16,128,512]{4,3,2,1,0:T(8,128)(2,1)S(1)} copy-done((bf16[1,2,16,128,512]{4,3,2,1,0:T(8,128)(2,1)S(1)}, bf16[1,2,16,128,512]{4,3,2,1,0:T(8,128)(2,1)}, u32[]{:S(2)}) %copy-start.1) | copy-done | bytes 4194328
  108.9 4.4 %slot_side.1 = bf16[2,16,128,512]{3,2,1,0:T(8,128)(2,1)} custom-call(s32[449]{0:T(512)S(1)} %pad_add_fusion.meta_ref, bf16[16,16,32,128]{3,2,1,0:T(8,128)(2,1)S(1)} %all_to_all.25.stripes_ref, bf16[2,16,128,512]{3,2,1,0:T(8,128)(2,1)S(1)} %bitcast.27, f32[256,4,128]{2,1,0:T(4,128)S(1)} %bitcast.32, f32[2,128]{1,0:T(2,128)S(1)} %reshape.84.sink_ref, ...), custom_call_target="tpu_custom_call" | custom-call | flops 536870912 | bytes 7342852 | tf_op jit(solution)/shard_map/slot_side/pallas_call | solution.py:259
  113.3 0.5 add.45
  113.8 0.9 join.1
  (18 shorter events, 0.1 us)
Async XLA Ops:
  0.6 9.5 %copy-start.2 = (s32[1,128]{1,0:T(1,128)S(1)}, s32[1,128]{1,0:T(1,128)}, u32[]{:S(2)}) copy-start(s32[1,128]{1,0:T(1,128)} %param.9) | copy-start | bytes 1540
  0.6 10.2 %copy-start.3 = (s32[1,64]{1,0:T(1,128)S(1)}, s32[1,64]{1,0:T(1,128)}, u32[]{:S(2)}) copy-start(s32[1,64]{1,0:T(1,128)} %param.10) | copy-start | bytes 772
  0.7 10.6 %copy-start.4 = (f32[4]{0:T(128)S(1)}, f32[4]{0:T(128)}, u32[]{:S(2)}) copy-start(f32[4]{0:T(128)} %param.8) | copy-start | bytes 52
  2.5 18.1 %all-to-all-start = ((bf16[16,4,32,128]{3,2,1,0:T(8,128)(2,1)}), bf16[16,4,32,128]{3,2,1,0:T(8,128)(2,1)S(1)}, u32[]{:S(2)}, u32[]{:S(2)}) async-start(bf16[16,4,32,128]{3,2,1,0:T(8,128)(2,1)} %bitcast.36), calls=%async_computation | async-start | bytes 1048576 | tf_op jit(solution)/shard_map/all_to_all | solution.py:254
  21.6 30.2 %copy-start = (bf16[1,2,16,128,512]{4,3,2,1,0:T(8,128)(2,1)S(1)}, bf16[1,2,16,128,512]{4,3,2,1,0:T(8,128)(2,1)}, u32[]{:S(2)}) copy-start(bf16[1,2,16,128,512]{4,3,2,1,0:T(8,128)(2,1)} %param.7) | copy-start | bytes 12582916
  96.7 17.1 %all-to-all-start.4 = ((bf16[16,4,32,128]{3,2,1,0:T(8,128)(2,1)}), bf16[16,4,32,128]{3,2,1,0:T(8,128)(2,1)S(1)}, u32[]{:S(2)}, u32[]{:S(2)}) async-start(bf16[16,4,32,128]{3,2,1,0:T(8,128)(2,1)} %bitcast.34), calls=%async_computation.4 | async-start | bytes 1048576 | tf_op jit(solution)/shard_map/all_to_all | solution.py:254
  101.5 11.8 %collective-permute-start = (f32[4]{0:T(128)S(1)}, f32[4]{0:T(128)S(1)}, u32[]{:S(2)}, u32[]{:S(2)}) collective-permute-start(f32[4]{0:T(128)S(1)} %reduce_sum.35), channel_id=1, source_target_pairs={{0,1},{1,0},{2,3},{3,2},{4,5},{5,4},{6,7},{7,6},{8,9},{9,8},{10,11... | collective-permute-start | bytes 56 | tf_op jit(solution)/shard_map/ppermute | solution.py:367
  106.7 2.2 %copy-start.1 = (bf16[1,2,16,128,512]{4,3,2,1,0:T(8,128)(2,1)S(1)}, bf16[1,2,16,128,512]{4,3,2,1,0:T(8,128)(2,1)}, u32[]{:S(2)}) copy-start(bf16[1,2,16,128,512]{4,3,2,1,0:T(8,128)(2,1)} %param.7) | copy-start | bytes 12582916

commit v4 on v3

--- a/solution.py
+++ b/solution.py
@@ -15,12 +15,16 @@
 SCALE = HD ** (-0.5)
 MIB = 1024 * 1024
 STEPS = 2
+GROUPS = 16
+PLACES, LIVE = GROUPS, GROUPS + 1
 IN_VMEM = pl.BlockSpec(memory_space=pltpu.VMEM)
 IN_HBM = pl.BlockSpec(memory_space=pltpu.HBM)
 IN_SMEM = pl.BlockSpec(memory_space=pltpu.SMEM)
 
 
-def cut_stripes(query_hbm, grad_hbm, out_hbm, rows_ref, out_ref, in_sems, out_sems):
+def cut_stripes(query_hbm, grad_hbm, turn_ref, out_hbm, done_ref, *scratch):
+    rows_ref, out_ref, in_sems, out_sems = scratch
+    done_ref[...] = jnp.zeros_like(done_ref)
     whiches, heads, halves, spans = out_ref.shape[:4]
     loads, stores = [], []
     for which, ref in enumerate((query_hbm, grad_hbm)):
@@ -55,19 +59,19 @@
 
 
 def spread_spans(meta_ref, in_ref, sink_ref, out_ref):
-    def body(i, carry):
-        out_ref[i] = in_ref[meta_ref[i] & 63]
+    def body(group, carry):
+        for slot in range(GROUPS):
+            out_ref[group, slot] = in_ref[meta_ref[group, slot] & 63]
         return carry
 
-    lax.fori_loop(0, out_ref.shape[0], body, 0, unroll=16)
-
-
-def add_partials(meta_ref, in_ref, out_ref, *, pos_at):
-
+    lax.fori_loop(0, out_ref.shape[0], body, 0)
+
+
+def add_partials(meta_ref, in_ref, out_ref):
     def body(span, carry):
-        here = pos_at + 2 * span - NB
-        left = in_ref[meta_ref[here]].astype(jnp.float32)
-        right = in_ref[meta_ref[here + 1]].astype(jnp.float32)
+        here = 2 * span - NB
+        left = in_ref[meta_ref[PLACES, here]].astype(jnp.float32)
+        right = in_ref[meta_ref[PLACES, here + 1]].astype(jnp.float32)
         out_ref[span] = (left + right).astype(jnp.bfloat16)
         return carry
 
@@ -129,22 +133,23 @@
     return top + jnp.log(total), deltas, part_s / total
 
 
-def slot_stats(meta_ref, stats_ref, sink_ref, slot, me_at):
-    mine_at = meta_ref[me_at] + slot
-    code = meta_ref[mine_at]
+def slot_stats(meta_ref, stats_ref, sink_ref, slot):
+    group = lax.axis_index("seq")
+    mine_at = group * GROUPS + slot
+    code = meta_ref[group, slot]
     live = ((code >> 6) & 1).astype(jnp.float32)
     log_total, deltas, _ = joined(stats_ref[mine_at], stats_ref[code >> 7], sink_ref[...])
     return log_total, deltas, live
 
 
 def token_side(
-    meta_ref, stripes_ref, enc_ref, stats_ref, sink_ref, out_ref, weights_ref, scores_ref, *, me_at
+    meta_ref, stripes_ref, enc_ref, stats_ref, sink_ref, out_ref, weights_ref, scores_ref
 ):
     heads = enc_ref.shape[3] // HD
     pairs = heads // 2
     slots = enc_ref.shape[1]
     for slot in range(slots):
-        log_total, deltas, live = slot_stats(meta_ref, stats_ref, sink_ref, slot, me_at)
+        log_total, deltas, live = slot_stats(meta_ref, stats_ref, sink_ref, slot)
         spare = jnp.zeros((8 - 2 * pairs, 2 * CH), jnp.float32)
         columns = jnp.concatenate([log_total, deltas, spare], axis=0).T
         for pair in range(pairs):
@@ -171,7 +176,7 @@
 
 
 def slot_side(
-    meta_ref, stripes_ref, enc_ref, stats_ref, sink_ref, after_ref, *refs, me_at
+    meta_ref, stripes_ref, enc_ref, stats_ref, sink_ref, after_ref, *refs
 ):
     out_ref, weights_ref, scores_ref = refs
     heads = enc_ref.shape[3] // HD
@@ -180,7 +185,7 @@
     first = pl.program_id(0) * count
     for step in range(count):
         slot = first + step
-        log_total, deltas, live = slot_stats(meta_ref, stats_ref, sink_ref, slot, me_at)
+        log_total, deltas, live = slot_stats(meta_ref, stats_ref, sink_ref, slot)
         for pair in range(pairs):
             cols = slice(pair * 2 * HD, (pair + 1) * 2 * HD)
             queries = paired(stripes_ref, 0, pair, slot, heads)
@@ -201,50 +206,67 @@
                 out_ref[which, step, :, cols] = rows.astype(jnp.bfloat16)
 
 
-def sink_side(meta_ref, stats_ref, sink_ref, after_ref, out_ref, *, pos_at, live_at, spans):
+def sink_side(meta_ref, stats_ref, sink_ref, after_ref, out_ref, *, spans):
     sink = sink_ref[...]
 
     def body(span, total):
-        here = pos_at + 2 * span - NB
-        live = meta_ref[live_at + span].astype(jnp.float32)
-        _, deltas, part = joined(stats_ref[meta_ref[here]], stats_ref[meta_ref[here + 1]], sink)
+        here = 2 * span - NB
+        live = meta_ref[LIVE, span].astype(jnp.float32)
+        left, right = stats_ref[meta_ref[PLACES, here]], stats_ref[meta_ref[PLACES, here + 1]]
+        _, deltas, part = joined(left, right, sink)
         return total - part * deltas * live
 
     out_ref[...] = lax.fori_loop(1, spans, body, jnp.zeros_like(sink), unroll=7)
 
 
-def routing(owner_row, doc_row, seq_index, slots, seq_count):
-    neigh_count, spans = owner_row.shape[0], doc_row.shape[0]
-    neigh_ids = jnp.arange(neigh_count, dtype=jnp.int32)
-    before = neigh_ids[None, :] < neigh_ids[:, None]
-    same_owner = owner_row[None, :] == owner_row[:, None]
-    slot_of = jnp.sum(before & same_owner, axis=1).astype(jnp.int32)
-    place = owner_row * slots + slot_of
-    other = jnp.flip(place.reshape(spans, NB), axis=1).reshape(-1)
-    span_ids = jnp.arange(spans, dtype=jnp.int32)
-    live = ((span_ids >= 1) & (doc_row == 0)).astype(jnp.int32)
-    next_live = jnp.concatenate([live[1:], jnp.zeros((1,), jnp.int32)])
-    reader = jnp.minimum(neigh_ids // NB + 1, spans - 1)
-    code = reader + 64 * jnp.repeat(next_live, NB) + 128 * other
-    flat = jnp.arange(slots * seq_count, dtype=jnp.int32)
-    codes = jnp.sum(jnp.where(place[None, :] == flat[:, None], code[None, :], 0), axis=1)
-    first = (seq_index * slots).astype(jnp.int32).reshape(1)
-    return jnp.concatenate([codes, place, live, first])
+def route(owner_ref, doc_ref, sink_ref, after_ref, meta_ref, rows_ref):
+    f32, i32 = jnp.float32, jnp.int32
+    groups, neighs, spans = GROUPS, owner_ref.shape[1], doc_ref.shape[1]
+
+    def ids(shape, dim):
+        return lax.broadcasted_iota(i32, shape, dim)
+
+    def one_hot(hits):
+        return hits.astype(f32).astype(jnp.bfloat16)
+
+    owner = owner_ref[...]
+    in_group = one_hot(ids((groups, neighs), 0) == owner)
+    earlier = one_hot(ids((neighs, neighs), 0) < ids((neighs, neighs), 1))
+    rank = dot(in_group, earlier, 1, 0) * in_group.astype(f32)
+    slot = jnp.sum(rank, axis=0, keepdims=True).astype(i32)
+    place = owner * groups + slot
+    lane = ids((1, neighs), 1)
+    other = jnp.where(lane % 2 == 0, pltpu.roll(place, neighs - 1, 1), pltpu.roll(place, 1, 1))
+    reader = lane // NB + 1
+    span = ids((1, spans), 1)
+    live = ((span >= 1) & (doc_ref[...] == 0)).astype(f32)
+    reads = one_hot(ids((spans, neighs), 0) == ids((spans, neighs), 1) // NB + 1)
+    read_live = dot(live.astype(jnp.bfloat16), reads, 1, 0)
+    low = jnp.minimum(reader, spans - 1).astype(f32) + 64.0 * read_live
+    in_slot = one_hot(ids((groups, neighs), 0) == slot)
+
+    def by_slot(row):
+        return dot(in_group * row.astype(jnp.bfloat16), in_slot, 1, 1).astype(i32)
+
+    codes = by_slot(low) + 128 * by_slot(other.astype(f32))
+    meta_ref[...] = jnp.zeros_like(meta_ref)
+    meta_ref[0:groups, 0:groups] = codes
+    meta_ref[groups : groups + 1] = place
+    meta_ref[groups + 1 : groups + 2, 0:spans] = live.astype(i32)
+    left = ids((1, 2 * CH), 1) < CH
+    for pair in range(rows_ref.shape[0]):
+        rows_ref[pair : pair + 1] = jnp.where(left, sink_ref[2 * pair], sink_ref[2 * pair + 1])
 
 
 def on_device(queries, encodings, sink, owner, doc_start, d_out):
     seq_count = lax.axis_size("seq")
-    seq_index = lax.axis_index("seq")
     tokens, width = queries.shape[1:]
     spans_here = tokens // CH
     heads = width // HD
     pairs = heads // 2
     slots = encodings.shape[2]
-    spans, neighs = doc_start.shape[1], owner.shape[1]
+    spans = doc_start.shape[1]
     places = seq_count * slots
-    pos_at = places
-    live_at = pos_at + neighs
-    me_at = live_at + spans
     bf16 = jnp.bfloat16
     f32 = jnp.float32
     stripe = (HALF, HD)
@@ -269,8 +291,6 @@
             **kw,
         )(*(in_hbm(x) if spec is IN_HBM else x for x, spec in zip(operands, in_specs)))
 
-    meta = routing(owner[0], doc_start[0], seq_index, slots, seq_count)
-    sink_rows = jnp.repeat(sink.reshape(pairs, 2), CH, axis=1)
     enc = encodings[0]
 
     def struct(shape, dtype=bf16):
@@ -283,15 +303,18 @@
         block = tuple(n // STEPS if d == axis else n for d, n in enumerate(shape))
         return pl.BlockSpec(block, lambda i: tuple(i if d == axis else 0 for d in range(len(shape))))
 
+    pairs_of_first = [(2 * i, 2 * (i ^ 1)) for i in range(seq_count)]
+    turn = lax.ppermute(sink, ("seq", "dp"), pairs_of_first)
     cut_shape = (2, heads, 2, spans_here) + stripe
-    cut = call(
+    cut, done = call(
         cut_stripes,
         "cut",
-        pltpu.HBM(cut_shape, bf16),
+        [pltpu.HBM(cut_shape, bf16), struct((8, HD), f32)],
         queries[0],
         d_out[0],
-        in_specs=[IN_HBM, IN_HBM],
-        out_specs=IN_HBM,
+        turn,
+        in_specs=[IN_HBM, IN_HBM, IN_VMEM],
+        out_specs=[IN_HBM, IN_VMEM],
         scratch_shapes=[
             pltpu.VMEM((2, tokens, width), bf16),
             pltpu.VMEM(cut_shape, bf16),
@@ -299,16 +322,27 @@
             pltpu.SemaphoreType.DMA((2,)),
         ],
     )
+    meta, sink_rows = call(
+        route,
+        "route",
+        [struct((24, HD), jnp.int32), struct((pairs, HD), f32)],
+        owner,
+        doc_start,
+        sink,
+        done,
+        in_specs=[IN_VMEM, IN_VMEM, IN_SMEM, IN_VMEM],
+        out_specs=[IN_VMEM, IN_VMEM],
+    )
     all_spans = everywhere(cut.reshape((seq_count, spans_here) + stripe))
     spread = call(
         spread_spans,
         "spread",
-        struct((places,) + stripe),
+        struct((seq_count, slots) + stripe),
         meta,
         all_spans.reshape((spans,) + stripe),
         sink_rows,
     )
-    stripes = everywhere(spread.reshape((seq_count, slots) + stripe))
+    stripes = everywhere(spread)
 
     stats_shape = (seq_count, slots, heads, HD)
     stats = call(
@@ -324,7 +358,7 @@
     all_stats = everywhere(stats).reshape(places, heads, HD)
     whole = (meta, stripes, enc, all_stats, sink_rows)
     partials = call(
-        functools.partial(token_side, me_at=me_at),
+        token_side,
         "token_side",
         struct(stripes.shape),
         *whole,
@@ -333,7 +367,7 @@
     )
     returned = everywhere(partials).reshape((places,) + stripe)
     summed = call(
-        functools.partial(add_partials, pos_at=pos_at),
+        add_partials,
         "add_partials",
         pltpu.HBM((spans,) + stripe, bf16),
         meta,
@@ -341,7 +375,7 @@
     )
     final = everywhere(summed.reshape((seq_count, spans_here) + stripe))
     enc_grads = call(
-        functools.partial(slot_side, me_at=me_at),
+        slot_side,
         "slot_side",
         struct(enc.shape),
         *whole,
@@ -353,7 +387,7 @@
         scratch_shapes=[pltpu.VMEM((slots // STEPS * pairs, NL, NL), bf16)] * 2,
     )
     sink_lanes = call(
-        functools.partial(sink_side, pos_at=pos_at, live_at=live_at, spans=spans),
+        functools.partial(sink_side, spans=spans),
         "sink_side",
         struct((pairs, HD), f32),
         meta,

time: 115 us -> 110 us (0.957)
  blocking collectives: 68.8 us -> 57.9 us
  starting transfers between devices: 16.4 us -> 22.5 us
  waiting for transfers between devices: 8.92 us -> 6.16 us
  Pallas kernels: 15.3 us -> 17.3 us
    all_to_all x3, blocking collectives: 68.8 us -> 57.9 us  [everywhere(): return lax.all_to_all(block, 'seq', split_axis=0, concat_axis=0, tiled=True)]
    ppermute x1, starting transfers between devices: 5.22 us -> 10.6 us  [on_device(): sink_total = sink_part + lax.ppermute(sink_part, 'dp', [(0, 1), (1, 0)])]
    all_to_all x2, waiting for transfers between devices: 8.91 us -> 6.15 us  [everywhere(): return lax.all_to_all(block, 'seq', split_axis=0, concat_axis=0, tiled=True)]
    pallas_call x8 -> x9, Pallas kernels: 15.3 us -> 17.3 us  [call(): pl.pallas_call(kernel, in_specs=in_specs, out_specs=out_specs, out_shape=...]
    unnamed x10, local copies, waits for them, and re-layouts: 2.21 us -> 4.15 us
  transfers between devices with their start and end apart: 3 -> 4, of which waited for: 1 -> 1; matrix products, arithmetic and copies ran while one was open for 2% -> 1% of each run, Pallas kernels for 5% -> 6%
where the time goes in v4:
time: 110 us; the launch traced here: 109 us
  blocking collectives  57.9 us (53%)
  starting transfers between devices  22.5 us (20%)
  Pallas kernels  17.3 us (16%)
  waiting for transfers between devices  6.16 us (6%)
  local copies, waits for them, and re-layouts  4.24 us (4%)
    all_to_all x3, blocking collectives, everywhere(): return lax.all_to_all(block, 'seq', split_axis=0, concat_axis=0, tiled=True)  57.9 us
    pallas_call x9, Pallas kernels, call(): pl.pallas_call(kernel, in_specs=in_specs, out_specs=out_specs, out_shape=...  17.3 us
    all_to_all x2, starting transfers between devices, everywhere(): return lax.all_to_all(block, 'seq', split_axis=0, concat_axis=0, tiled=True)  11.2 us
    ppermute x1, starting transfers between devices, on_device(): sink_total = sink_part + lax.ppermute(sink_part, 'dp', [(0, 1), (1, 0)])  10.6 us
    all_to_all x2, waiting for transfers between devices, everywhere(): return lax.all_to_all(block, 'seq', split_axis=0, concat_axis=0, tiled=True)  6.15 us
    unnamed x10, local copies, waits for them, and re-layouts  4.15 us
  transfers between devices with their start and end apart: 4, of which 1 were waited for; matrix products, arithmetic and copies ran while one was open for 1% of the time, Pallas kernels for 6%

profile of v4, /device:TPU:1, one launch (start us, length us, event | category | flops | bytes accessed | tf_op | source)
XLA Modules:
  0.0 109.5 jit_solution(18438226692568457979)
XLA Ops:
  0.6 0.7 collective-permute-start
  1.3 0.0 collective-permute-done.turn_ref
  1.3 1.8 %cut.1 = (bf16[2,4,2,4,32,128]{5,4,3,2,1,0:T(8,128)(2,1)}, f32[8,128]{1,0:T(8,128)S(1)}) custom-call(bf16[256,512]{1,0:T(8,128)(2,1)} %bitcast.22, bf16[256,512]{1,0:T(8,128)(2,1)} %bitcast.23, f32[4]{0:T(128)S(1)} %collective-permute-done.turn_ref), custom_call_target="tpu_custom_call" | custom-call | bytes 524304 | tf_op jit(solution)/shard_map/cut/pallas_call | solution.py:281
  3.1 7.6 %all-to-all-start = ((bf16[16,4,32,128]{3,2,1,0:T(8,128)(2,1)}), bf16[16,4,32,128]{3,2,1,0:T(8,128)(2,1)S(1)}, u32[]{:S(2)}, u32[]{:S(2)}) async-start(bf16[16,4,32,128]{3,2,1,0:T(8,128)(2,1)} %bitcast.21), calls=%async_computation | async-start | bytes 1048576 | tf_op jit(solution)/shard_map/all_to_all | solution.py:276
  10.7 0.0 copy-start.2
  10.8 0.6 copy-done.2
  11.4 0.0 copy-start.3
  11.4 0.7 copy-done.3
  12.1 0.0 copy-start.4
  12.1 0.7 copy-done.4
  12.7 0.9 route.1
  13.6 6.1 %all-to-all-done = bf16[16,4,32,128]{3,2,1,0:T(8,128)(2,1)S(1)} async-done(((bf16[16,4,32,128]{3,2,1,0:T(8,128)(2,1)}), bf16[16,4,32,128]{3,2,1,0:T(8,128)(2,1)S(1)}, u32[]{:S(2)}, u32[]{:S(2)}) %all-to-all-start) | async-done | bytes 524320 | tf_op jit(solution)/shard_map/all_to_all | solution.py:276
  19.7 1.1 %spread.1 = bf16[16,16,32,128]{3,2,1,0:T(8,128)(2,1)S(1)} custom-call(s32[24,128]{1,0:T(8,128)S(1)} %get-tuple-element.11.meta_ref, bf16[64,32,128]{2,1,0:T(8,128)(2,1)S(1)} %bitcast.18, f32[2,128]{1,0:T(2,128)S(1)} %get-tuple-element.13.sink_ref), custom_call_target="tpu_custom_call" | custom-call | bytes 537600 | tf_op jit(solution)/shard_map/spread/pallas_call | solution.py:281
  20.9 0.0 copy-start
  20.9 24.5 %all_to_all.25.stripes_ref = bf16[16,16,32,128]{3,2,1,0:T(8,128)(2,1)S(1)} all-to-all(bf16[16,16,32,128]{3,2,1,0:T(8,128)(2,1)S(1)} %spread.1), channel_id=1, replica_groups=mesh['seq'=16,'mp'=8,'dp'=2] {'seq'}, dimensions={0} | all-to-all | bytes 4194304 | tf_op jit(solution)/shard_map/all_to_all | solution.py:276
  45.4 0.0 copy-done
  45.4 1.6 %stats.1 = f32[16,16,4,128]{3,2,1,0:T(4,128)S(1)} custom-call(bf16[16,16,32,128]{3,2,1,0:T(8,128)(2,1)S(1)} %all_to_all.25.stripes_ref, bf16[2,16,128,512]{3,2,1,0:T(8,128)(2,1)S(1)} %bitcast.11), custom_call_target="tpu_custom_call" | custom-call | flops 268435456 | bytes 6291456 | tf_op jit(solution)/shard_map/stats/pallas_call | solution.py:281
  47.1 11.6 %all_to_all.26 = f32[16,16,4,128]{3,2,1,0:T(4,128)S(1)} all-to-all(f32[16,16,4,128]{3,2,1,0:T(4,128)S(1)} %stats.1), channel_id=1, replica_groups=mesh['seq'=16,'mp'=8,'dp'=2] {'seq'}, dimensions={0} | all-to-all | bytes 1048576 | tf_op jit(solution)/shard_map/all_to_all | solution.py:276
  58.7 3.2 %token_side.1 = bf16[16,16,32,128]{3,2,1,0:T(8,128)(2,1)S(1)} custom-call(s32[24,128]{1,0:T(8,128)S(1)} %get-tuple-element.11.meta_ref, bf16[16,16,32,128]{3,2,1,0:T(8,128)(2,1)S(1)} %all_to_all.25.stripes_ref, bf16[2,16,128,512]{3,2,1,0:T(8,128)(2,1)S(1)} %bitcast.12, f32[256,4,128]{2,1,0:T(4,128)S(1)} %bitcast.14, f32[2,128]{1,0:T(2,128)S(1)} %get-tuple-element.13.sink_ref), custom_call_target="tpu_custom_call" | custom-call | flops 536870912 | bytes 6829056 | tf_op jit(solution)/shard_map/token_side/pallas_call | solution.py:281
  61.9 21.8 %all_to_all.27 = bf16[16,16,32,128]{3,2,1,0:T(8,128)(2,1)S(1)} all-to-all(bf16[16,16,32,128]{3,2,1,0:T(8,128)(2,1)S(1)} %token_side.1), channel_id=1, replica_groups=mesh['seq'=16,'mp'=8,'dp'=2] {'seq'}, dimensions={0} | all-to-all | bytes 4194304 | tf_op jit(solution)/shard_map/all_to_all | solution.py:276
  83.7 1.9 %add_partials.1.after_ref = bf16[64,32,128]{2,1,0:T(8,128)(2,1)} custom-call(s32[24,128]{1,0:T(8,128)S(1)} %get-tuple-element.11.meta_ref, bf16[256,32,128]{2,1,0:T(8,128)(2,1)S(1)} %bitcast.17), custom_call_target="tpu_custom_call" | custom-call | bytes 2109440 | tf_op jit(solution)/shard_map/add_partials/pallas_call | solution.py:281
  85.6 3.6 %all-to-all-start.4 = ((bf16[16,4,32,128]{3,2,1,0:T(8,128)(2,1)}), bf16[16,4,32,128]{3,2,1,0:T(8,128)(2,1)S(1)}, u32[]{:S(2)}, u32[]{:S(2)}) async-start(bf16[16,4,32,128]{3,2,1,0:T(8,128)(2,1)} %bitcast.19), calls=%async_computation.4 | async-start | bytes 1048576 | tf_op jit(solution)/shard_map/all_to_all | solution.py:276
  89.1 1.3 %sink_side.1 = f32[2,128]{1,0:T(2,128)S(1)} custom-call(s32[24,128]{1,0:T(8,128)S(1)} %get-tuple-element.11.meta_ref, f32[256,4,128]{2,1,0:T(4,128)S(1)} %bitcast.15, f32[2,128]{1,0:T(2,128)S(1)} %get-tuple-element.13.sink_ref, bf16[64,32,128]{2,1,0:T(8,128)(2,1)} %add_partials.1.after_ref), custom_call_target="tpu_custom_call" | custom-call | flops 262144 | bytes 1061888 | tf_op jit(solution)/shard_map/sink_side/pallas_call | solution.py:281
  90.4 0.1 reshape.31
  90.5 0.1 reduce_sum.9
  90.7 10.6 %collective-permute-start.1 = (f32[4]{0:T(128)S(1)}, f32[4]{0:T(128)S(1)}, u32[]{:S(2)}, u32[]{:S(2)}) collective-permute-start(f32[4]{0:T(128)S(1)} %reduce_sum.9), channel_id=1, source_target_pairs={{0,1},{1,0},{2,3},{3,2},{4,5},{5,4},{6,7},{7,6},{8,9},{9,8},{10,11... | collective-permute-start | bytes 56 | tf_op jit(solution)/shard_map/ppermute | solution.py:401
  101.3 2.2 %copy-done.1 = bf16[1,2,16,128,512]{4,3,2,1,0:T(8,128)(2,1)S(1)} copy-done((bf16[1,2,16,128,512]{4,3,2,1,0:T(8,128)(2,1)S(1)}, bf16[1,2,16,128,512]{4,3,2,1,0:T(8,128)(2,1)}, u32[]{:S(2)}) %copy-start.1) | copy-done | bytes 4194328
  103.5 4.6 %slot_side.1 = bf16[2,16,128,512]{3,2,1,0:T(8,128)(2,1)} custom-call(s32[24,128]{1,0:T(8,128)S(1)} %get-tuple-element.11.meta_ref, bf16[16,16,32,128]{3,2,1,0:T(8,128)(2,1)S(1)} %all_to_all.25.stripes_ref, bf16[2,16,128,512]{3,2,1,0:T(8,128)(2,1)S(1)} %bitcast.13, f32[256,4,128]{2,1,0:T(4,128)S(1)} %bitcast.16, f32[2,128]{1,0:T(2,128)S(1)} %get-tuple-element.13.sink_ref, ...), custom_call_target="tpu_custom_call" | custom-call | flops 536870912 | bytes 7353344 | tf_op jit(solution)/shard_map/slot_side/pallas_call | solution.py:281
  108.1 0.0 collective-permute-done.1
  108.1 0.5 add.3
  108.6 0.0 all-to-all-done.4.in_ref
  108.6 0.9 join.1
  (1 shorter events, 0.0 us)
Async XLA Ops:
  0.6 0.7 collective-permute-start
  3.1 16.6 %all-to-all-start = ((bf16[16,4,32,128]{3,2,1,0:T(8,128)(2,1)}), bf16[16,4,32,128]{3,2,1,0:T(8,128)(2,1)S(1)}, u32[]{:S(2)}, u32[]{:S(2)}) async-start(bf16[16,4,32,128]{3,2,1,0:T(8,128)(2,1)} %bitcast.21), calls=%async_computation | async-start | bytes 1048576 | tf_op jit(solution)/shard_map/all_to_all | solution.py:276
  10.7 0.7 copy-start.2
  11.4 0.7 copy-start.3
  12.1 0.7 copy-start.4
  20.9 24.6 %copy-start = (bf16[1,2,16,128,512]{4,3,2,1,0:T(8,128)(2,1)S(1)}, bf16[1,2,16,128,512]{4,3,2,1,0:T(8,128)(2,1)}, u32[]{:S(2)}) copy-start(bf16[1,2,16,128,512]{4,3,2,1,0:T(8,128)(2,1)} %param.7) | copy-start | bytes 12582916
  85.6 23.0 %all-to-all-start.4 = ((bf16[16,4,32,128]{3,2,1,0:T(8,128)(2,1)}), bf16[16,4,32,128]{3,2,1,0:T(8,128)(2,1)S(1)}, u32[]{:S(2)}, u32[]{:S(2)}) async-start(bf16[16,4,32,128]{3,2,1,0:T(8,128)(2,1)} %bitcast.19), calls=%async_computation.4 | async-start | bytes 1048576 | tf_op jit(solution)/shard_map/all_to_all | solution.py:276
  90.7 17.4 %collective-permute-start.1 = (f32[4]{0:T(128)S(1)}, f32[4]{0:T(128)S(1)}, u32[]{:S(2)}, u32[]{:S(2)}) collective-permute-start(f32[4]{0:T(128)S(1)} %reduce_sum.9), channel_id=1, source_target_pairs={{0,1},{1,0},{2,3},{3,2},{4,5},{5,4},{6,7},{7,6},{8,9},{9,8},{10,11... | collective-permute-start | bytes 56 | tf_op jit(solution)/shard_map/ppermute | solution.py:401
  101.3 2.2 %copy-start.1 = (bf16[1,2,16,128,512]{4,3,2,1,0:T(8,128)(2,1)S(1)}, bf16[1,2,16,128,512]{4,3,2,1,0:T(8,128)(2,1)}, u32[]{:S(2)}) copy-start(bf16[1,2,16,128,512]{4,3,2,1,0:T(8,128)(2,1)} %param.7) | copy-start | bytes 12582916

commit v5 on v4

--- a/solution.py
+++ b/solution.py
@@ -59,24 +59,17 @@
 
 
 def spread_spans(meta_ref, in_ref, sink_ref, out_ref):
-    def body(group, carry):
+    for group in range(GROUPS):
         for slot in range(GROUPS):
             out_ref[group, slot] = in_ref[meta_ref[group, slot] & 63]
-        return carry
-
-    lax.fori_loop(0, out_ref.shape[0], body, 0)
 
 
 def add_partials(meta_ref, in_ref, out_ref):
-    def body(span, carry):
-        here = 2 * span - NB
-        left = in_ref[meta_ref[PLACES, here]].astype(jnp.float32)
-        right = in_ref[meta_ref[PLACES, here + 1]].astype(jnp.float32)
+    out_ref[0] = jnp.zeros(out_ref.shape[1:], jnp.bfloat16)
+    for span in range(1, out_ref.shape[0]):
+        left = in_ref[meta_ref[PLACES, NB * span - 2]].astype(jnp.float32)
+        right = in_ref[meta_ref[PLACES, NB * span - 1]].astype(jnp.float32)
         out_ref[span] = (left + right).astype(jnp.bfloat16)
-        return carry
-
-    out_ref[0] = jnp.zeros(out_ref.shape[1:], jnp.bfloat16)
-    lax.fori_loop(1, out_ref.shape[0], body, 0, unroll=9)
 
 
 def paired(stripes_ref, which, pair, slot, heads):
@@ -303,7 +296,7 @@
         block = tuple(n // STEPS if d == axis else n for d, n in enumerate(shape))
         return pl.BlockSpec(block, lambda i: tuple(i if d == axis else 0 for d in range(len(shape))))
 
-    pairs_of_first = [(2 * i, 2 * (i ^ 1)) for i in range(seq_count)]
+    pairs_of_first = [(2 * i, 2 * (i ^ 2)) for i in range(seq_count)]
     turn = lax.ppermute(sink, ("seq", "dp"), pairs_of_first)
     cut_shape = (2, heads, 2, spans_here) + stripe
     cut, done = call(

time: 110 us -> 109 us (level)
  blocking collectives: 57.9 us -> 54.8 us
  starting transfers between devices: 22.5 us -> 25.1 us
    all_to_all x3, blocking collectives: 57.9 us -> 54.8 us  [everywhere(): return lax.all_to_all(block, 'seq', split_axis=0, concat_axis=0, tiled=True)]
    ppermute x1, starting transfers between devices: 10.6 us -> 13.2 us  [on_device(): sink_total = sink_part + lax.ppermute(sink_part, 'dp', [(0, 1), (1, 0)])]
where the time goes in v5:
time: 109 us
  blocking collectives  54.8 us (50%)
  starting transfers between devices  25.1 us (23%)
  Pallas kernels  17 us (16%)
  waiting for transfers between devices  6.16 us (6%)
  local copies, waits for them, and re-layouts  4.24 us (4%)
    all_to_all x3, blocking collectives, everywhere(): return lax.all_to_all(block, 'seq', split_axis=0, concat_axis=0, tiled=True)  54.8 us
    pallas_call x9, Pallas kernels, call(): pl.pallas_call(kernel, in_specs=in_specs, out_specs=out_specs, out_shape=...  17 us
    ppermute x1, starting transfers between devices, on_device(): sink_total = sink_part + lax.ppermute(sink_part, 'dp', [(0, 1), (1, 0)])  13.2 us
    all_to_all x2, starting transfers between devices, everywhere(): return lax.all_to_all(block, 'seq', split_axis=0, concat_axis=0, tiled=True)  11.2 us
    all_to_all x2, waiting for transfers between devices, everywhere(): return lax.all_to_all(block, 'seq', split_axis=0, concat_axis=0, tiled=True)  6.15 us
    unnamed x10, local copies, waits for them, and re-layouts  4.15 us
  transfers between devices with their start and end apart: 4, of which 1 were waited for; matrix products, arithmetic and copies ran while one was open for 1% of the time, Pallas kernels for 6%

profile of v5, /device:TPU:1, one launch (start us, length us, event | category | flops | bytes accessed | tf_op | source)
XLA Modules:
  0.0 108.5 jit_solution(7610158279257327034)
XLA Ops:
  0.6 0.7 collective-permute-start
  1.3 0.0 collective-permute-done.turn_ref
  1.3 1.8 %cut.1 = (bf16[2,4,2,4,32,128]{5,4,3,2,1,0:T(8,128)(2,1)}, f32[8,128]{1,0:T(8,128)S(1)}) custom-call(bf16[256,512]{1,0:T(8,128)(2,1)} %bitcast.22, bf16[256,512]{1,0:T(8,128)(2,1)} %bitcast.23, f32[4]{0:T(128)S(1)} %collective-permute-done.turn_ref), custom_call_target="tpu_custom_call" | custom-call | bytes 524304 | tf_op jit(solution)/shard_map/cut/pallas_call | solution.py:274
  3.1 7.6 %all-to-all-start = ((bf16[16,4,32,128]{3,2,1,0:T(8,128)(2,1)}), bf16[16,4,32,128]{3,2,1,0:T(8,128)(2,1)S(1)}, u32[]{:S(2)}, u32[]{:S(2)}) async-start(bf16[16,4,32,128]{3,2,1,0:T(8,128)(2,1)} %bitcast.21), calls=%async_computation | async-start | bytes 1048576 | tf_op jit(solution)/shard_map/all_to_all | solution.py:269
  10.7 0.0 copy-start.2
  10.8 0.6 copy-done.2
  11.4 0.0 copy-start.3
  11.4 0.7 copy-done.3
  12.1 0.7 copy-done.4
  12.7 0.9 route.1
  13.6 6.1 %all-to-all-done = bf16[16,4,32,128]{3,2,1,0:T(8,128)(2,1)S(1)} async-done(((bf16[16,4,32,128]{3,2,1,0:T(8,128)(2,1)}), bf16[16,4,32,128]{3,2,1,0:T(8,128)(2,1)S(1)}, u32[]{:S(2)}, u32[]{:S(2)}) %all-to-all-start) | async-done | bytes 524320 | tf_op jit(solution)/shard_map/all_to_all | solution.py:269
  19.7 1.0 spread.1
  20.7 0.0 copy-start
  20.8 22.8 %all_to_all.25.stripes_ref = bf16[16,16,32,128]{3,2,1,0:T(8,128)(2,1)S(1)} all-to-all(bf16[16,16,32,128]{3,2,1,0:T(8,128)(2,1)S(1)} %spread.1), channel_id=1, replica_groups=mesh['seq'=16,'mp'=8,'dp'=2] {'seq'}, dimensions={0} | all-to-all | bytes 4194304 | tf_op jit(solution)/shard_map/all_to_all | solution.py:269
  43.5 0.0 copy-done
  43.5 1.6 %stats.1 = f32[16,16,4,128]{3,2,1,0:T(4,128)S(1)} custom-call(bf16[16,16,32,128]{3,2,1,0:T(8,128)(2,1)S(1)} %all_to_all.25.stripes_ref, bf16[2,16,128,512]{3,2,1,0:T(8,128)(2,1)S(1)} %bitcast.11), custom_call_target="tpu_custom_call" | custom-call | flops 268435456 | bytes 6291456 | tf_op jit(solution)/shard_map/stats/pallas_call | solution.py:274
  45.1 11.6 %all_to_all.26 = f32[16,16,4,128]{3,2,1,0:T(4,128)S(1)} all-to-all(f32[16,16,4,128]{3,2,1,0:T(4,128)S(1)} %stats.1), channel_id=1, replica_groups=mesh['seq'=16,'mp'=8,'dp'=2] {'seq'}, dimensions={0} | all-to-all | bytes 1048576 | tf_op jit(solution)/shard_map/all_to_all | solution.py:269
  56.8 3.2 %token_side.1 = bf16[16,16,32,128]{3,2,1,0:T(8,128)(2,1)S(1)} custom-call(s32[24,128]{1,0:T(8,128)S(1)} %get-tuple-element.11.meta_ref, bf16[16,16,32,128]{3,2,1,0:T(8,128)(2,1)S(1)} %all_to_all.25.stripes_ref, bf16[2,16,128,512]{3,2,1,0:T(8,128)(2,1)S(1)} %bitcast.12, f32[256,4,128]{2,1,0:T(4,128)S(1)} %bitcast.14, f32[2,128]{1,0:T(2,128)S(1)} %get-tuple-element.13.sink_ref), custom_call_target="tpu_custom_call" | custom-call | flops 536870912 | bytes 6829056 | tf_op jit(solution)/shard_map/token_side/pallas_call | solution.py:274
  60.0 20.4 %all_to_all.27 = bf16[16,16,32,128]{3,2,1,0:T(8,128)(2,1)S(1)} all-to-all(bf16[16,16,32,128]{3,2,1,0:T(8,128)(2,1)S(1)} %token_side.1), channel_id=1, replica_groups=mesh['seq'=16,'mp'=8,'dp'=2] {'seq'}, dimensions={0} | all-to-all | bytes 4194304 | tf_op jit(solution)/shard_map/all_to_all | solution.py:269
  80.4 1.6 %add_partials.1.after_ref = bf16[64,32,128]{2,1,0:T(8,128)(2,1)} custom-call(s32[24,128]{1,0:T(8,128)S(1)} %get-tuple-element.11.meta_ref, bf16[256,32,128]{2,1,0:T(8,128)(2,1)S(1)} %bitcast.17), custom_call_target="tpu_custom_call" | custom-call | bytes 2109440 | tf_op jit(solution)/shard_map/add_partials/pallas_call | solution.py:274
  82.0 3.6 %all-to-all-start.4 = ((bf16[16,4,32,128]{3,2,1,0:T(8,128)(2,1)}), bf16[16,4,32,128]{3,2,1,0:T(8,128)(2,1)S(1)}, u32[]{:S(2)}, u32[]{:S(2)}) async-start(bf16[16,4,32,128]{3,2,1,0:T(8,128)(2,1)} %bitcast.19), calls=%async_computation.4 | async-start | bytes 1048576 | tf_op jit(solution)/shard_map/all_to_all | solution.py:269
  85.6 1.3 %sink_side.1 = f32[2,128]{1,0:T(2,128)S(1)} custom-call(s32[24,128]{1,0:T(8,128)S(1)} %get-tuple-element.11.meta_ref, f32[256,4,128]{2,1,0:T(4,128)S(1)} %bitcast.15, f32[2,128]{1,0:T(2,128)S(1)} %get-tuple-element.13.sink_ref, bf16[64,32,128]{2,1,0:T(8,128)(2,1)} %add_partials.1.after_ref), custom_call_target="tpu_custom_call" | custom-call | flops 262144 | bytes 1061888 | tf_op jit(solution)/shard_map/sink_side/pallas_call | solution.py:274
  86.9 0.1 reshape.31
  87.0 0.1 reduce_sum.9
  87.1 13.2 %collective-permute-start.1 = (f32[4]{0:T(128)S(1)}, f32[4]{0:T(128)S(1)}, u32[]{:S(2)}, u32[]{:S(2)}) collective-permute-start(f32[4]{0:T(128)S(1)} %reduce_sum.9), channel_id=1, source_target_pairs={{0,1},{1,0},{2,3},{3,2},{4,5},{5,4},{6,7},{7,6},{8,9},{9,8},{10,11... | collective-permute-start | bytes 56 | tf_op jit(solution)/shard_map/ppermute | solution.py:394
  100.4 0.0 copy-start.1
  100.4 2.2 %copy-done.1 = bf16[1,2,16,128,512]{4,3,2,1,0:T(8,128)(2,1)S(1)} copy-done((bf16[1,2,16,128,512]{4,3,2,1,0:T(8,128)(2,1)S(1)}, bf16[1,2,16,128,512]{4,3,2,1,0:T(8,128)(2,1)}, u32[]{:S(2)}) %copy-start.1) | copy-done | bytes 4194328
  102.5 4.6 %slot_side.1 = bf16[2,16,128,512]{3,2,1,0:T(8,128)(2,1)} custom-call(s32[24,128]{1,0:T(8,128)S(1)} %get-tuple-element.11.meta_ref, bf16[16,16,32,128]{3,2,1,0:T(8,128)(2,1)S(1)} %all_to_all.25.stripes_ref, bf16[2,16,128,512]{3,2,1,0:T(8,128)(2,1)S(1)} %bitcast.13, f32[256,4,128]{2,1,0:T(4,128)S(1)} %bitcast.16, f32[2,128]{1,0:T(2,128)S(1)} %get-tuple-element.13.sink_ref, ...), custom_call_target="tpu_custom_call" | custom-call | flops 536870912 | bytes 7353344 | tf_op jit(solution)/shard_map/slot_side/pallas_call | solution.py:274
  107.1 0.0 collective-permute-done.1
  107.1 0.5 add.3
  107.6 0.0 all-to-all-done.4.in_ref
  107.6 0.9 join.1
  (1 shorter events, 0.0 us)
Async XLA Ops:
  0.6 0.7 collective-permute-start
  3.1 16.6 %all-to-all-start = ((bf16[16,4,32,128]{3,2,1,0:T(8,128)(2,1)}), bf16[16,4,32,128]{3,2,1,0:T(8,128)(2,1)S(1)}, u32[]{:S(2)}, u32[]{:S(2)}) async-start(bf16[16,4,32,128]{3,2,1,0:T(8,128)(2,1)} %bitcast.21), calls=%async_computation | async-start | bytes 1048576 | tf_op jit(solution)/shard_map/all_to_all | solution.py:269
  10.7 0.7 copy-start.2
  11.4 0.7 copy-start.3
  12.1 0.7 copy-start.4
  20.7 22.8 %copy-start = (bf16[1,2,16,128,512]{4,3,2,1,0:T(8,128)(2,1)S(1)}, bf16[1,2,16,128,512]{4,3,2,1,0:T(8,128)(2,1)}, u32[]{:S(2)}) copy-start(bf16[1,2,16,128,512]{4,3,2,1,0:T(8,128)(2,1)} %param.7) | copy-start | bytes 12582916
  82.0 25.6 %all-to-all-start.4 = ((bf16[16,4,32,128]{3,2,1,0:T(8,128)(2,1)}), bf16[16,4,32,128]{3,2,1,0:T(8,128)(2,1)S(1)}, u32[]{:S(2)}, u32[]{:S(2)}) async-start(bf16[16,4,32,128]{3,2,1,0:T(8,128)(2,1)} %bitcast.19), calls=%async_computation.4 | async-start | bytes 1048576 | tf_op jit(solution)/shard_map/all_to_all | solution.py:269
  87.1 20.0 %collective-permute-start.1 = (f32[4]{0:T(128)S(1)}, f32[4]{0:T(128)S(1)}, u32[]{:S(2)}, u32[]{:S(2)}) collective-permute-start(f32[4]{0:T(128)S(1)} %reduce_sum.9), channel_id=1, source_target_pairs={{0,1},{1,0},{2,3},{3,2},{4,5},{5,4},{6,7},{7,6},{8,9},{9,8},{10,11... | collective-permute-start | bytes 56 | tf_op jit(solution)/shard_map/ppermute | solution.py:394
  100.4 2.2 %copy-start.1 = (bf16[1,2,16,128,512]{4,3,2,1,0:T(8,128)(2,1)S(1)}, bf16[1,2,16,128,512]{4,3,2,1,0:T(8,128)(2,1)}, u32[]{:S(2)}) copy-start(bf16[1,2,16,128,512]{4,3,2,1,0:T(8,128)(2,1)} %param.7) | copy-start | bytes 12582916

commit v6 on v5

--- a/solution.py
+++ b/solution.py
@@ -25,24 +25,26 @@
 def cut_stripes(query_hbm, grad_hbm, turn_ref, out_hbm, done_ref, *scratch):
     rows_ref, out_ref, in_sems, out_sems = scratch
     done_ref[...] = jnp.zeros_like(done_ref)
-    whiches, heads, halves, spans = out_ref.shape[:4]
+    _, heads, halves, spans = out_ref.shape[:4]
+    steps = [(which, span) for which in range(2) for span in range(0, spans, 2)]
     loads, stores = [], []
-    for which, ref in enumerate((query_hbm, grad_hbm)):
-        loads.append(pltpu.make_async_copy(ref, rows_ref.at[which], in_sems.at[which]))
-        stores.append(
-            pltpu.make_async_copy(out_ref.at[which], out_hbm.at[which], out_sems.at[which])
-        )
-        loads[which].start()
-    for which in range(whiches):
-        loads[which].wait()
+    for step, (which, span) in enumerate(steps):
+        rows = pl.ds(span * CH, 2 * CH)
+        source = (query_hbm, grad_hbm)[which].at[rows]
+        loads.append(pltpu.make_async_copy(source, rows_ref.at[which, rows], in_sems.at[step]))
+        loads[step].start()
+    for step, (which, first) in enumerate(steps):
+        loads[step].wait()
         for head in range(heads):
             for half in range(halves):
-                for span in range(spans):
+                for span in (first, first + 1):
                     row = span * CH + half * HALF
                     out_ref[which, head, half, span] = rows_ref[
                         which, row : row + HALF, head * HD : (head + 1) * HD
                     ]
-        stores[which].start()
+        at = (which, slice(None), slice(None), pl.ds(first, 2))
+        stores.append(pltpu.make_async_copy(out_ref.at[at], out_hbm.at[at], out_sems.at[step]))
+        stores[step].start()
     for store in stores:
         store.wait()
 
@@ -96,10 +98,7 @@
 def stats_of(stripes_ref, enc_ref, out_ref):
     heads = enc_ref.shape[3] // HD
     pairs = heads // 2
-    count = out_ref.shape[1]
-    first = pl.program_id(0) * count
-    for step in range(count):
-        slot = first + step
+    for slot in range(out_ref.shape[1]):
         for pair in range(pairs):
             cols = slice(pair * 2 * HD, (pair + 1) * 2 * HD)
             queries = paired(stripes_ref, 0, pair, slot, heads)
@@ -109,9 +108,9 @@
             top = jnp.max(scores, axis=0, keepdims=True)
             powers = jnp.exp(scores - top)
             total = jnp.sum(powers, axis=0, keepdims=True)
-            out_ref[0, step, pair : pair + 1] = top + jnp.log(total)
+            out_ref[0, slot, pair : pair + 1] = top + jnp.log(total)
             delta = jnp.sum(powers * d_weights, axis=0, keepdims=True) / total
-            out_ref[0, step, pairs + pair : pairs + pair + 1] = delta
+            out_ref[0, slot, pairs + pair : pairs + pair + 1] = delta
     for dest in range(1, out_ref.shape[0]):
         out_ref[dest] = out_ref[0]
 
@@ -311,8 +310,8 @@
         scratch_shapes=[
             pltpu.VMEM((2, tokens, width), bf16),
             pltpu.VMEM(cut_shape, bf16),
-            pltpu.SemaphoreType.DMA((2,)),
-            pltpu.SemaphoreType.DMA((2,)),
+            pltpu.SemaphoreType.DMA((spans_here,)),
+            pltpu.SemaphoreType.DMA((spans_here,)),
         ],
     )
     meta, sink_rows = call(
@@ -344,8 +343,6 @@
         struct(stats_shape, f32),
         stripes,
         enc,
-        grid=(STEPS,),
-        out_specs=by_slots(stats_shape, 1),
         work=flops,
     )
     all_stats = everywhere(stats).reshape(places, heads, HD)

time: 109 us -> 108 us (level)
  no operation moved by 1% of the time
where the time goes in v6:
time: 108 us
  blocking collectives  54.9 us (51%)
  starting transfers between devices  24.4 us (23%)
  Pallas kernels  16.7 us (15%)
  waiting for transfers between devices  6.16 us (6%)
  local copies, waits for them, and re-layouts  4.24 us (4%)
    all_to_all x3, blocking collectives, everywhere(): return lax.all_to_all(block, 'seq', split_axis=0, concat_axis=0, tiled=True)  54.9 us
    pallas_call x9, Pallas kernels, call(): pl.pallas_call(kernel, in_specs=in_specs, out_specs=out_specs, out_shape=...  16.7 us
    ppermute x1, starting transfers between devices, on_device(): sink_total = sink_part + lax.ppermute(sink_part, 'dp', [(0, 1), (1, 0)])  12.5 us
    all_to_all x2, starting transfers between devices, everywhere(): return lax.all_to_all(block, 'seq', split_axis=0, concat_axis=0, tiled=True)  11.2 us
    all_to_all x2, waiting for transfers between devices, everywhere(): return lax.all_to_all(block, 'seq', split_axis=0, concat_axis=0, tiled=True)  6.15 us
    unnamed x10, local copies, waits for them, and re-layouts  4.15 us
  transfers between devices with their start and end apart: 4, of which 1 were waited for; matrix products, arithmetic and copies ran while one was open for 1% of the time, Pallas kernels for 6%

profile of v6, /device:TPU:1, one launch (start us, length us, event | category | flops | bytes accessed | tf_op | source)
XLA Modules:
  0.0 107.8 jit_solution(12566610445842790345)
XLA Ops:
  0.6 0.7 collective-permute-start
  1.3 0.0 collective-permute-done.turn_ref
  1.3 1.8 %cut.1 = (bf16[2,4,2,4,32,128]{5,4,3,2,1,0:T(8,128)(2,1)}, f32[8,128]{1,0:T(8,128)S(1)}) custom-call(bf16[256,512]{1,0:T(8,128)(2,1)} %bitcast.22, bf16[256,512]{1,0:T(8,128)(2,1)} %bitcast.23, f32[4]{0:T(128)S(1)} %collective-permute-done.turn_ref), custom_call_target="tpu_custom_call" | custom-call | bytes 524304 | tf_op jit(solution)/shard_map/cut/pallas_call | solution.py:273
  3.2 7.6 %all-to-all-start = ((bf16[16,4,32,128]{3,2,1,0:T(8,128)(2,1)}), bf16[16,4,32,128]{3,2,1,0:T(8,128)(2,1)S(1)}, u32[]{:S(2)}, u32[]{:S(2)}) async-start(bf16[16,4,32,128]{3,2,1,0:T(8,128)(2,1)} %bitcast.21), calls=%async_computation | async-start | bytes 1048576 | tf_op jit(solution)/shard_map/all_to_all | solution.py:268
  10.8 0.0 copy-start.2
  10.8 0.6 copy-done.2
  11.4 0.0 copy-start.3
  11.4 0.7 copy-done.3
  12.1 0.0 copy-start.4
  12.1 0.7 copy-done.4
  12.7 0.9 route.1
  13.6 6.1 %all-to-all-done = bf16[16,4,32,128]{3,2,1,0:T(8,128)(2,1)S(1)} async-done(((bf16[16,4,32,128]{3,2,1,0:T(8,128)(2,1)}), bf16[16,4,32,128]{3,2,1,0:T(8,128)(2,1)S(1)}, u32[]{:S(2)}, u32[]{:S(2)}) %all-to-all-start) | async-done | bytes 524320 | tf_op jit(solution)/shard_map/all_to_all | solution.py:268
  19.8 1.0 spread.1
  20.8 0.0 copy-start
  20.8 22.8 %all_to_all.25.stripes_ref = bf16[16,16,32,128]{3,2,1,0:T(8,128)(2,1)S(1)} all-to-all(bf16[16,16,32,128]{3,2,1,0:T(8,128)(2,1)S(1)} %spread.1), channel_id=1, replica_groups=mesh['seq'=16,'mp'=8,'dp'=2] {'seq'}, dimensions={0} | all-to-all | bytes 4194304 | tf_op jit(solution)/shard_map/all_to_all | solution.py:268
  43.5 0.0 copy-done
  43.5 1.4 %stats.1 = f32[16,16,4,128]{3,2,1,0:T(4,128)S(1)} custom-call(bf16[16,16,32,128]{3,2,1,0:T(8,128)(2,1)S(1)} %all_to_all.25.stripes_ref, bf16[2,16,128,512]{3,2,1,0:T(8,128)(2,1)S(1)} %bitcast.11), custom_call_target="tpu_custom_call" | custom-call | flops 268435456 | bytes 6291456 | tf_op jit(solution)/shard_map/stats/pallas_call | solution.py:273
  44.9 11.6 %all_to_all.26 = f32[16,16,4,128]{3,2,1,0:T(4,128)S(1)} all-to-all(f32[16,16,4,128]{3,2,1,0:T(4,128)S(1)} %stats.1), channel_id=1, replica_groups=mesh['seq'=16,'mp'=8,'dp'=2] {'seq'}, dimensions={0} | all-to-all | bytes 1048576 | tf_op jit(solution)/shard_map/all_to_all | solution.py:268
  56.5 3.2 %token_side.1 = bf16[16,16,32,128]{3,2,1,0:T(8,128)(2,1)S(1)} custom-call(s32[24,128]{1,0:T(8,128)S(1)} %get-tuple-element.11.meta_ref, bf16[16,16,32,128]{3,2,1,0:T(8,128)(2,1)S(1)} %all_to_all.25.stripes_ref, bf16[2,16,128,512]{3,2,1,0:T(8,128)(2,1)S(1)} %bitcast.12, f32[256,4,128]{2,1,0:T(4,128)S(1)} %bitcast.14, f32[2,128]{1,0:T(2,128)S(1)} %get-tuple-element.13.sink_ref), custom_call_target="tpu_custom_call" | custom-call | flops 536870912 | bytes 6829056 | tf_op jit(solution)/shard_map/token_side/pallas_call | solution.py:273
  59.8 20.5 %all_to_all.27 = bf16[16,16,32,128]{3,2,1,0:T(8,128)(2,1)S(1)} all-to-all(bf16[16,16,32,128]{3,2,1,0:T(8,128)(2,1)S(1)} %token_side.1), channel_id=1, replica_groups=mesh['seq'=16,'mp'=8,'dp'=2] {'seq'}, dimensions={0} | all-to-all | bytes 4194304 | tf_op jit(solution)/shard_map/all_to_all | solution.py:268
  80.3 1.6 %add_partials.1.after_ref = bf16[64,32,128]{2,1,0:T(8,128)(2,1)} custom-call(s32[24,128]{1,0:T(8,128)S(1)} %get-tuple-element.11.meta_ref, bf16[256,32,128]{2,1,0:T(8,128)(2,1)S(1)} %bitcast.17), custom_call_target="tpu_custom_call" | custom-call | bytes 2109440 | tf_op jit(solution)/shard_map/add_partials/pallas_call | solution.py:273
  81.9 3.6 %all-to-all-start.4 = ((bf16[16,4,32,128]{3,2,1,0:T(8,128)(2,1)}), bf16[16,4,32,128]{3,2,1,0:T(8,128)(2,1)S(1)}, u32[]{:S(2)}, u32[]{:S(2)}) async-start(bf16[16,4,32,128]{3,2,1,0:T(8,128)(2,1)} %bitcast.19), calls=%async_computation.4 | async-start | bytes 1048576 | tf_op jit(solution)/shard_map/all_to_all | solution.py:268
  85.5 1.3 %sink_side.1 = f32[2,128]{1,0:T(2,128)S(1)} custom-call(s32[24,128]{1,0:T(8,128)S(1)} %get-tuple-element.11.meta_ref, f32[256,4,128]{2,1,0:T(4,128)S(1)} %bitcast.15, f32[2,128]{1,0:T(2,128)S(1)} %get-tuple-element.13.sink_ref, bf16[64,32,128]{2,1,0:T(8,128)(2,1)} %add_partials.1.after_ref), custom_call_target="tpu_custom_call" | custom-call | flops 262144 | bytes 1061888 | tf_op jit(solution)/shard_map/sink_side/pallas_call | solution.py:273
  86.8 0.1 reshape.31
  86.9 0.1 reduce_sum.9
  87.0 12.5 %collective-permute-start.1 = (f32[4]{0:T(128)S(1)}, f32[4]{0:T(128)S(1)}, u32[]{:S(2)}, u32[]{:S(2)}) collective-permute-start(f32[4]{0:T(128)S(1)} %reduce_sum.9), channel_id=1, source_target_pairs={{0,1},{1,0},{2,3},{3,2},{4,5},{5,4},{6,7},{7,6},{8,9},{9,8},{10,11... | collective-permute-start | bytes 56 | tf_op jit(solution)/shard_map/ppermute | solution.py:391
  99.6 2.2 %copy-done.1 = bf16[1,2,16,128,512]{4,3,2,1,0:T(8,128)(2,1)S(1)} copy-done((bf16[1,2,16,128,512]{4,3,2,1,0:T(8,128)(2,1)S(1)}, bf16[1,2,16,128,512]{4,3,2,1,0:T(8,128)(2,1)}, u32[]{:S(2)}) %copy-start.1) | copy-done | bytes 4194328
  101.8 4.6 %slot_side.1 = bf16[2,16,128,512]{3,2,1,0:T(8,128)(2,1)} custom-call(s32[24,128]{1,0:T(8,128)S(1)} %get-tuple-element.11.meta_ref, bf16[16,16,32,128]{3,2,1,0:T(8,128)(2,1)S(1)} %all_to_all.25.stripes_ref, bf16[2,16,128,512]{3,2,1,0:T(8,128)(2,1)S(1)} %bitcast.13, f32[256,4,128]{2,1,0:T(4,128)S(1)} %bitcast.16, f32[2,128]{1,0:T(2,128)S(1)} %get-tuple-element.13.sink_ref, ...), custom_call_target="tpu_custom_call" | custom-call | flops 536870912 | bytes 7353344 | tf_op jit(solution)/shard_map/slot_side/pallas_call | solution.py:273
  106.4 0.0 collective-permute-done.1
  106.4 0.5 add.3
  106.9 0.0 all-to-all-done.4.in_ref
  106.9 0.9 join.1
  (1 shorter events, 0.0 us)
Async XLA Ops:
  0.6 0.7 collective-permute-start
  3.2 16.6 %all-to-all-start = ((bf16[16,4,32,128]{3,2,1,0:T(8,128)(2,1)}), bf16[16,4,32,128]{3,2,1,0:T(8,128)(2,1)S(1)}, u32[]{:S(2)}, u32[]{:S(2)}) async-start(bf16[16,4,32,128]{3,2,1,0:T(8,128)(2,1)} %bitcast.21), calls=%async_computation | async-start | bytes 1048576 | tf_op jit(solution)/shard_map/all_to_all | solution.py:268
  10.8 0.7 copy-start.2
  11.4 0.7 copy-start.3
  12.1 0.7 copy-start.4
  20.8 22.8 %copy-start = (bf16[1,2,16,128,512]{4,3,2,1,0:T(8,128)(2,1)S(1)}, bf16[1,2,16,128,512]{4,3,2,1,0:T(8,128)(2,1)}, u32[]{:S(2)}) copy-start(bf16[1,2,16,128,512]{4,3,2,1,0:T(8,128)(2,1)} %param.7) | copy-start | bytes 12582916
  81.9 24.9 %all-to-all-start.4 = ((bf16[16,4,32,128]{3,2,1,0:T(8,128)(2,1)}), bf16[16,4,32,128]{3,2,1,0:T(8,128)(2,1)S(1)}, u32[]{:S(2)}, u32[]{:S(2)}) async-start(bf16[16,4,32,128]{3,2,1,0:T(8,128)(2,1)} %bitcast.19), calls=%async_computation.4 | async-start | bytes 1048576 | tf_op jit(solution)/shard_map/all_to_all | solution.py:268
  87.0 19.3 %collective-permute-start.1 = (f32[4]{0:T(128)S(1)}, f32[4]{0:T(128)S(1)}, u32[]{:S(2)}, u32[]{:S(2)}) collective-permute-start(f32[4]{0:T(128)S(1)} %reduce_sum.9), channel_id=1, source_target_pairs={{0,1},{1,0},{2,3},{3,2},{4,5},{5,4},{6,7},{7,6},{8,9},{9,8},{10,11... | collective-permute-start | bytes 56 | tf_op jit(solution)/shard_map/ppermute | solution.py:391
  99.6 2.2 %copy-start.1 = (bf16[1,2,16,128,512]{4,3,2,1,0:T(8,128)(2,1)S(1)}, bf16[1,2,16,128,512]{4,3,2,1,0:T(8,128)(2,1)}, u32[]{:S(2)}) copy-start(bf16[1,2,16,128,512]{4,3,2,1,0:T(8,128)(2,1)} %param.7) | copy-start | bytes 12582916

commit v7 on v6

--- a/solution.py
+++ b/solution.py
@@ -49,15 +49,22 @@
         store.wait()
 
 
-def join_stripes(in_ref, attended_ref, query_ref):
-    spans, heads = in_ref.shape[1], attended_ref.shape[1] // HD
-    for which, ref in enumerate((attended_ref, query_ref)):
+def join_stripes(in_ref, attended_hbm, query_hbm, rows_ref, sems):
+    spans, heads = in_ref.shape[1], rows_ref.shape[2] // HD
+    copies = []
+    for which, target in enumerate((attended_hbm, query_hbm)):
         for head in range(heads):
             for half in range(2):
                 stripe = (which * heads + head) * 2 + half
                 for span in range(spans):
                     row = span * CH + half * HALF
-                    ref[row : row + HALF, head * HD : (head + 1) * HD] = in_ref[stripe, span]
+                    rows_ref[which, row : row + HALF, head * HD : (head + 1) * HD] = in_ref[
+                        stripe, span
+                    ]
+        copies.append(pltpu.make_async_copy(rows_ref.at[which], target, sems.at[which]))
+        copies[which].start()
+    for copy in copies:
+        copy.wait()
 
 
 def spread_spans(meta_ref, in_ref, sink_ref, out_ref):
@@ -66,12 +73,24 @@
             out_ref[group, slot] = in_ref[meta_ref[group, slot] & 63]
 
 
-def add_partials(meta_ref, in_ref, out_ref):
-    out_ref[0] = jnp.zeros(out_ref.shape[1:], jnp.bfloat16)
-    for span in range(1, out_ref.shape[0]):
-        left = in_ref[meta_ref[PLACES, NB * span - 2]].astype(jnp.float32)
-        right = in_ref[meta_ref[PLACES, NB * span - 1]].astype(jnp.float32)
-        out_ref[span] = (left + right).astype(jnp.bfloat16)
+def add_partials(meta_ref, in_ref, out_hbm, out_ref, sems):
+    per_copy = out_ref.shape[0] // sems.shape[0]
+    copies = []
+    for span in range(out_ref.shape[0]):
+        if span == 0:
+            out_ref[0] = jnp.zeros(out_ref.shape[1:], jnp.bfloat16)
+        else:
+            left = in_ref[meta_ref[PLACES, NB * span - 2]].astype(jnp.float32)
+            right = in_ref[meta_ref[PLACES, NB * span - 1]].astype(jnp.float32)
+            out_ref[span] = (left + right).astype(jnp.bfloat16)
+        if span % per_copy == per_copy - 1:
+            at = pl.ds(len(copies) * per_copy, per_copy)
+            copies.append(
+                pltpu.make_async_copy(out_ref.at[at], out_hbm.at[at], sems.at[len(copies)])
+            )
+            copies[-1].start()
+    for copy in copies:
+        copy.wait()
 
 
 def paired(stripes_ref, which, pair, slot, heads):
@@ -362,6 +381,8 @@
         pltpu.HBM((spans,) + stripe, bf16),
         meta,
         returned,
+        out_specs=IN_HBM,
+        scratch_shapes=[pltpu.VMEM((spans,) + stripe, bf16), pltpu.SemaphoreType.DMA((4,))],
     )
     final = everywhere(summed.reshape((seq_count, spans_here) + stripe))
     enc_grads = call(
@@ -390,9 +411,13 @@
     sink_part = jnp.sum(sink_lanes.reshape(heads, CH), axis=1)
     sink_total = sink_part + lax.ppermute(sink_part, "dp", [(0, 1), (1, 0)])
 
-    rows = pl.BlockSpec((tokens, width), lambda: (0, 0))
     attended, grad_query = call(
-        join_stripes, "join", [struct((tokens, width))] * 2, final, out_specs=[rows, rows]
+        join_stripes,
+        "join",
+        [pltpu.HBM((tokens, width), bf16)] * 2,
+        final,
+        out_specs=[IN_HBM, IN_HBM],
+        scratch_shapes=[pltpu.VMEM((2, tokens, width), bf16), pltpu.SemaphoreType.DMA((2,))],
     )
     return attended[None], grad_query[None], enc_grads[None], sink_total
 

time: 108 us -> 108 us (level)
  no operation moved by 1% of the time
where the time goes in v7:
time: 108 us
  blocking collectives  54.9 us (51%)
  starting transfers between devices  24.4 us (23%)
  Pallas kernels  16.6 us (15%)
  waiting for transfers between devices  6.16 us (6%)
  local copies, waits for them, and re-layouts  4.24 us (4%)
    all_to_all x3, blocking collectives, everywhere(): return lax.all_to_all(block, 'seq', split_axis=0, concat_axis=0, tiled=True)  54.9 us
    pallas_call x9, Pallas kernels, call(): pl.pallas_call(kernel, in_specs=in_specs, out_specs=out_specs, out_shape=...  16.6 us
    ppermute x1, starting transfers between devices, on_device(): sink_total = sink_part + lax.ppermute(sink_part, 'dp', [(0, 1), (1, 0)])  12.6 us
    all_to_all x2, starting transfers between devices, everywhere(): return lax.all_to_all(block, 'seq', split_axis=0, concat_axis=0, tiled=True)  11.2 us
    all_to_all x2, waiting for transfers between devices, everywhere(): return lax.all_to_all(block, 'seq', split_axis=0, concat_axis=0, tiled=True)  6.15 us
    unnamed x10, local copies, waits for them, and re-layouts  4.15 us
  transfers between devices with their start and end apart: 4, of which 1 were waited for; matrix products, arithmetic and copies ran while one was open for 1% of the time, Pallas kernels for 6%

profile of v7, /device:TPU:1, one launch (start us, length us, event | category | flops | bytes accessed | tf_op | source)
XLA Modules:
  0.0 107.7 jit_solution(697646227983294804)
XLA Ops:
  0.6 0.7 collective-permute-start
  1.3 0.0 collective-permute-done.turn_ref
  1.3 1.8 %cut.1 = (bf16[2,4,2,4,32,128]{5,4,3,2,1,0:T(8,128)(2,1)}, f32[8,128]{1,0:T(8,128)S(1)}) custom-call(bf16[256,512]{1,0:T(8,128)(2,1)} %bitcast.22, bf16[256,512]{1,0:T(8,128)(2,1)} %bitcast.23, f32[4]{0:T(128)S(1)} %collective-permute-done.turn_ref), custom_call_target="tpu_custom_call" | custom-call | bytes 524304 | tf_op jit(solution)/shard_map/cut/pallas_call | solution.py:292
  3.2 7.6 %all-to-all-start = ((bf16[16,4,32,128]{3,2,1,0:T(8,128)(2,1)}), bf16[16,4,32,128]{3,2,1,0:T(8,128)(2,1)S(1)}, u32[]{:S(2)}, u32[]{:S(2)}) async-start(bf16[16,4,32,128]{3,2,1,0:T(8,128)(2,1)} %bitcast.21), calls=%async_computation | async-start | bytes 1048576 | tf_op jit(solution)/shard_map/all_to_all | solution.py:287
  10.8 0.0 copy-start.2
  10.8 0.6 copy-done.2
  11.4 0.0 copy-start.3
  11.4 0.7 copy-done.3
  12.1 0.0 copy-start.4
  12.1 0.7 copy-done.4
  12.7 0.9 route.1
  13.6 6.1 %all-to-all-done = bf16[16,4,32,128]{3,2,1,0:T(8,128)(2,1)S(1)} async-done(((bf16[16,4,32,128]{3,2,1,0:T(8,128)(2,1)}), bf16[16,4,32,128]{3,2,1,0:T(8,128)(2,1)S(1)}, u32[]{:S(2)}, u32[]{:S(2)}) %all-to-all-start) | async-done | bytes 524320 | tf_op jit(solution)/shard_map/all_to_all | solution.py:287
  19.8 1.0 spread.1
  20.8 0.0 copy-start
  20.8 22.8 %all_to_all.25.stripes_ref = bf16[16,16,32,128]{3,2,1,0:T(8,128)(2,1)S(1)} all-to-all(bf16[16,16,32,128]{3,2,1,0:T(8,128)(2,1)S(1)} %spread.1), channel_id=1, replica_groups=mesh['seq'=16,'mp'=8,'dp'=2] {'seq'}, dimensions={0} | all-to-all | bytes 4194304 | tf_op jit(solution)/shard_map/all_to_all | solution.py:287
  43.5 0.0 copy-done
  43.5 1.4 %stats.1 = f32[16,16,4,128]{3,2,1,0:T(4,128)S(1)} custom-call(bf16[16,16,32,128]{3,2,1,0:T(8,128)(2,1)S(1)} %all_to_all.25.stripes_ref, bf16[2,16,128,512]{3,2,1,0:T(8,128)(2,1)S(1)} %bitcast.11), custom_call_target="tpu_custom_call" | custom-call | flops 268435456 | bytes 6291456 | tf_op jit(solution)/shard_map/stats/pallas_call | solution.py:292
  44.9 11.6 %all_to_all.26 = f32[16,16,4,128]{3,2,1,0:T(4,128)S(1)} all-to-all(f32[16,16,4,128]{3,2,1,0:T(4,128)S(1)} %stats.1), channel_id=1, replica_groups=mesh['seq'=16,'mp'=8,'dp'=2] {'seq'}, dimensions={0} | all-to-all | bytes 1048576 | tf_op jit(solution)/shard_map/all_to_all | solution.py:287
  56.5 3.2 %token_side.1 = bf16[16,16,32,128]{3,2,1,0:T(8,128)(2,1)S(1)} custom-call(s32[24,128]{1,0:T(8,128)S(1)} %get-tuple-element.11.meta_ref, bf16[16,16,32,128]{3,2,1,0:T(8,128)(2,1)S(1)} %all_to_all.25.stripes_ref, bf16[2,16,128,512]{3,2,1,0:T(8,128)(2,1)S(1)} %bitcast.12, f32[256,4,128]{2,1,0:T(4,128)S(1)} %bitcast.14, f32[2,128]{1,0:T(2,128)S(1)} %get-tuple-element.13.sink_ref), custom_call_target="tpu_custom_call" | custom-call | flops 536870912 | bytes 6829056 | tf_op jit(solution)/shard_map/token_side/pallas_call | solution.py:292
  59.8 20.5 %all_to_all.27 = bf16[16,16,32,128]{3,2,1,0:T(8,128)(2,1)S(1)} all-to-all(bf16[16,16,32,128]{3,2,1,0:T(8,128)(2,1)S(1)} %token_side.1), channel_id=1, replica_groups=mesh['seq'=16,'mp'=8,'dp'=2] {'seq'}, dimensions={0} | all-to-all | bytes 4194304 | tf_op jit(solution)/shard_map/all_to_all | solution.py:287
  80.3 1.6 %add_partials.1.after_ref = bf16[64,32,128]{2,1,0:T(8,128)(2,1)} custom-call(s32[24,128]{1,0:T(8,128)S(1)} %get-tuple-element.11.meta_ref, bf16[256,32,128]{2,1,0:T(8,128)(2,1)S(1)} %bitcast.17), custom_call_target="tpu_custom_call" | custom-call | bytes 2109440 | tf_op jit(solution)/shard_map/add_partials/pallas_call | solution.py:292
  81.9 3.6 %all-to-all-start.4 = ((bf16[16,4,32,128]{3,2,1,0:T(8,128)(2,1)}), bf16[16,4,32,128]{3,2,1,0:T(8,128)(2,1)S(1)}, u32[]{:S(2)}, u32[]{:S(2)}) async-start(bf16[16,4,32,128]{3,2,1,0:T(8,128)(2,1)} %bitcast.19), calls=%async_computation.4 | async-start | bytes 1048576 | tf_op jit(solution)/shard_map/all_to_all | solution.py:287
  85.5 1.3 %sink_side.1 = f32[2,128]{1,0:T(2,128)S(1)} custom-call(s32[24,128]{1,0:T(8,128)S(1)} %get-tuple-element.11.meta_ref, f32[256,4,128]{2,1,0:T(4,128)S(1)} %bitcast.15, f32[2,128]{1,0:T(2,128)S(1)} %get-tuple-element.13.sink_ref, bf16[64,32,128]{2,1,0:T(8,128)(2,1)} %add_partials.1.after_ref), custom_call_target="tpu_custom_call" | custom-call | flops 262144 | bytes 1061888 | tf_op jit(solution)/shard_map/sink_side/pallas_call | solution.py:292
  86.8 0.1 reshape.31
  86.9 0.1 reduce_sum.9
  87.0 12.6 %collective-permute-start.1 = (f32[4]{0:T(128)S(1)}, f32[4]{0:T(128)S(1)}, u32[]{:S(2)}, u32[]{:S(2)}) collective-permute-start(f32[4]{0:T(128)S(1)} %reduce_sum.9), channel_id=1, source_target_pairs={{0,1},{1,0},{2,3},{3,2},{4,5},{5,4},{6,7},{7,6},{8,9},{9,8},{10,11... | collective-permute-start | bytes 56 | tf_op jit(solution)/shard_map/ppermute | solution.py:412
  99.6 2.2 %copy-done.1 = bf16[1,2,16,128,512]{4,3,2,1,0:T(8,128)(2,1)S(1)} copy-done((bf16[1,2,16,128,512]{4,3,2,1,0:T(8,128)(2,1)S(1)}, bf16[1,2,16,128,512]{4,3,2,1,0:T(8,128)(2,1)}, u32[]{:S(2)}) %copy-start.1) | copy-done | bytes 4194328
  101.8 4.6 %slot_side.1 = bf16[2,16,128,512]{3,2,1,0:T(8,128)(2,1)} custom-call(s32[24,128]{1,0:T(8,128)S(1)} %get-tuple-element.11.meta_ref, bf16[16,16,32,128]{3,2,1,0:T(8,128)(2,1)S(1)} %all_to_all.25.stripes_ref, bf16[2,16,128,512]{3,2,1,0:T(8,128)(2,1)S(1)} %bitcast.13, f32[256,4,128]{2,1,0:T(4,128)S(1)} %bitcast.16, f32[2,128]{1,0:T(2,128)S(1)} %get-tuple-element.13.sink_ref, ...), custom_call_target="tpu_custom_call" | custom-call | flops 536870912 | bytes 7353344 | tf_op jit(solution)/shard_map/slot_side/pallas_call | solution.py:292
  106.4 0.0 collective-permute-done.1
  106.4 0.5 add.3
  106.9 0.0 all-to-all-done.4.in_ref
  106.9 0.9 join.1
  (1 shorter events, 0.0 us)
Async XLA Ops:
  0.6 0.7 collective-permute-start
  3.2 16.6 %all-to-all-start = ((bf16[16,4,32,128]{3,2,1,0:T(8,128)(2,1)}), bf16[16,4,32,128]{3,2,1,0:T(8,128)(2,1)S(1)}, u32[]{:S(2)}, u32[]{:S(2)}) async-start(bf16[16,4,32,128]{3,2,1,0:T(8,128)(2,1)} %bitcast.21), calls=%async_computation | async-start | bytes 1048576 | tf_op jit(solution)/shard_map/all_to_all | solution.py:287
  10.8 0.7 copy-start.2
  11.4 0.7 copy-start.3
  12.1 0.7 copy-start.4
  20.8 22.8 %copy-start = (bf16[1,2,16,128,512]{4,3,2,1,0:T(8,128)(2,1)S(1)}, bf16[1,2,16,128,512]{4,3,2,1,0:T(8,128)(2,1)}, u32[]{:S(2)}) copy-start(bf16[1,2,16,128,512]{4,3,2,1,0:T(8,128)(2,1)} %param.7) | copy-start | bytes 12582916
  81.9 25.0 %all-to-all-start.4 = ((bf16[16,4,32,128]{3,2,1,0:T(8,128)(2,1)}), bf16[16,4,32,128]{3,2,1,0:T(8,128)(2,1)S(1)}, u32[]{:S(2)}, u32[]{:S(2)}) async-start(bf16[16,4,32,128]{3,2,1,0:T(8,128)(2,1)} %bitcast.19), calls=%async_computation.4 | async-start | bytes 1048576 | tf_op jit(solution)/shard_map/all_to_all | solution.py:287
  87.0 19.4 %collective-permute-start.1 = (f32[4]{0:T(128)S(1)}, f32[4]{0:T(128)S(1)}, u32[]{:S(2)}, u32[]{:S(2)}) collective-permute-start(f32[4]{0:T(128)S(1)} %reduce_sum.9), channel_id=1, source_target_pairs={{0,1},{1,0},{2,3},{3,2},{4,5},{5,4},{6,7},{7,6},{8,9},{9,8},{10,11... | collective-permute-start | bytes 56 | tf_op jit(solution)/shard_map/ppermute | solution.py:412
  99.6 2.2 %copy-start.1 = (bf16[1,2,16,128,512]{4,3,2,1,0:T(8,128)(2,1)S(1)}, bf16[1,2,16,128,512]{4,3,2,1,0:T(8,128)(2,1)}, u32[]{:S(2)}) copy-start(bf16[1,2,16,128,512]{4,3,2,1,0:T(8,128)(2,1)} %param.7) | copy-start | bytes 12582916
